TPU v7x, 32 devices: a whole 2x2x4 slice. The times are simulated.
32 devices in a mesh: dp: 8 (over z, x), mp: 4 (over y, core).
Axes of the slice: x: 2, y: 2, z: 4, core: 2. Of those that a mesh axis runs over, the one named last changes fastest.
Arguments:
- input_ids: int32 [16, 512], P('dp'), may hold values from 0 to 6303
- seq_lengths: int32 [16, 4], P('dp'), may hold values from 0 to 512, as said below
- loss_positions: int32 [16, 80], P('dp'), may hold values from 0 to 511, as said below
- targets: int32 [16, 80], P('dp'), may hold values from 0 to 6303
- block_owner: int32 [192], replicated, may hold values from 0 to 191, as said below
- layer_master: float32 [4, 192, 128, 128], P('mp', 'dp')
- stats_left: float32 [4, 192, 128, 128], P('mp', 'dp'), as said below
- stats_right: float32 [4, 192, 128, 128], P('mp', 'dp'), as said below
- root_left: float32 [4, 192, 128, 128], P('mp', 'dp'), as said below
- root_right: float32 [4, 192, 128, 128], P('mp', 'dp'), as said below
- table_master: float32 [6304, 1024], P(('dp', 'mp')), may hold values from -0.36 to 0.36
- table_first: float32 [6304, 1024], P(('dp', 'mp')), may hold values from -1.2 to 1.2
- table_second: float32 [6304, 1024], P(('dp', 'mp')), may hold values from 0.01 to 0.1
- vector_master: float32 [526, 1024], replicated
- vector_first: float32 [526, 1024], replicated, may hold values from -1.2 to 1.2
- vector_second: float32 [526, 1024], replicated, may hold values from 0.01 to 0.1
Outputs:
- loss: float32 [], replicated
- grad_norm: float32 [], replicated
- layer_new: float32 [4, 192, 128, 128], P('mp', 'dp')
- left_new: float32 [4, 192, 128, 128], P('mp', 'dp')
- right_new: float32 [4, 192, 128, 128], P('mp', 'dp')
- table_new: float32 [6304, 1024], P(('dp', 'mp'))
- table_first_new: float32 [6304, 1024], P(('dp', 'mp'))
- table_second_new: float32 [6304, 1024], P(('dp', 'mp'))
- vector_new: float32 [526, 1024], replicated
- vector_first_new: float32 [526, 1024], replicated
- vector_second_new: float32 [526, 1024], replicated
Inputs may be any that keep to these rules, and one draw needn't show every extreme that they name: `seq_lengths`: each row packs its sequences from slot 0 on, each 128 to 512 long, unused slots 0 after the used ones, and the lengths sum to at most 512; the rest of the row is padding. `loss_positions`: distinct positions of one row, each below the sum of that row's lengths. `block_owner`: a permutation; device index i of dp owns the blocks at slots i * 24 to (i + 1) * 24 - 1. `stats_left`: symmetric. `stats_right`: symmetric. `root_left`: symmetric. `root_right`: symmetric.
All inputs are finite; a program needn't handle non-finite values.
Results may differ from a plain program's by a relative error of at most 0.00205.
The roundings to bfloat16 on the way count: a program that leaves them out, or rounds other values in their place, can miss the bound.
Values may be sent and summed in bfloat16 or wider, within the bound.
No kernel may reach another device: no remote copies, remote signals or barrier semaphores. Data moves between devices by JAX's collectives and lax.ppermute only.
A program may use at most 256 MiB of HBM per device.

v0:
```python
import math

import jax
import jax.numpy as jnp
from jax import lax
from jax.sharding import PartitionSpec as P

D = 1024
HEADS = 16
HD = 64
FF = 4096
VOC_DEV = 197
LEN = 512
MB = 2
POS = 80
KB = 128


HIGH = lax.Precision.HIGHEST
EPS_NORM = 1e-05
EPS_ADAM = 1e-08
BETA_FIRST = 0.5
BETA_SECOND = 0.5
RATE_ADAM = 0.01
RATE_SHAMPOO = 0.03
DECAY_TABLE = 0.01
DECAY_LAYER = 0.01
STAT_DECAY = 0.5
CLIP_FACTOR = 16.0
MASK_FILL = -1000000000.0


def joined_2(array, axis, combine):
    everything = jax.tree.map(lambda part: lax.all_gather(part, axis), array)
    initial = jax.tree.map(lambda part: part[0], everything)

    def hop(k, so_far):
        return combine(so_far, jax.tree.map(lambda part: part[k], everything))

    return lax.fori_loop(1, lax.axis_size(axis), hop, initial)


def gelu_exact(values):
    return 0.5 * values * (1.0 + jax.scipy.special.erf(values * 0.7071067811865476))


def gelu_slope(values):
    cumulative = 0.5 * (1.0 + jax.scipy.special.erf(values * 0.7071067811865476))
    density = jnp.exp(-0.5 * values * values) * 0.3989422804014327
    return cumulative + values * density


def norm_forward(values, norm_gain, norm_shift):
    row_mean = jnp.mean(values, axis=-1, keepdims=True)
    centered = values - row_mean
    variance = jnp.mean(centered * centered, axis=-1, keepdims=True)
    inv_dev = lax.rsqrt(variance + EPS_NORM)
    normed = centered * inv_dev
    return (normed * norm_gain + norm_shift, normed, inv_dev)


def norm_backward(grad_out, normed, inv_dev, norm_gain):
    scaled = grad_out * norm_gain
    grad_in = inv_dev * (
        scaled
        - jnp.mean(scaled, axis=-1, keepdims=True)
        - normed * jnp.mean(scaled * normed, axis=-1, keepdims=True)
    )
    return (grad_in, jnp.sum(grad_out * normed, axis=0), jnp.sum(grad_out, axis=0))


def positions_of(lengths, length):
    seq_ends = jnp.cumsum(lengths)
    places = jnp.arange(length, dtype=jnp.int32)
    passed = places[:, None] >= seq_ends[None, :]
    segment = jnp.sum(passed.astype(jnp.int32), axis=1)
    seq_start = jnp.max(jnp.where(passed, seq_ends[None, :], 0), axis=1)
    return (segment, places - seq_start)


def from_tiles(stacked, height, breadth, tile_size):
    arranged = stacked.reshape(height // tile_size, breadth // tile_size, tile_size, tile_size)
    return arranged.transpose(0, 2, 1, 3).reshape(height, breadth)


def to_tiles(matrix, tile_size):
    height, breadth = matrix.shape
    arranged = matrix.reshape(height // tile_size, tile_size, breadth // tile_size, tile_size)
    return arranged.transpose(0, 2, 1, 3).reshape(-1, tile_size, tile_size)


def split_pieces(stacked, model_width, inner_width, hidden, tile_size):
    first_end = model_width // tile_size * (3 * inner_width // tile_size)
    second_end = first_end + inner_width // tile_size * (model_width // tile_size)
    third_end = second_end + model_width // tile_size * (hidden // tile_size)
    joined = from_tiles(stacked[:first_end], model_width, 3 * inner_width, tile_size)
    output = from_tiles(stacked[first_end:second_end], inner_width, model_width, tile_size)
    upward = from_tiles(stacked[second_end:third_end], model_width, hidden, tile_size)
    downward = from_tiles(stacked[third_end:], hidden, model_width, tile_size)
    return (joined, output, upward, downward)


def adam_step(master, moment_one, moment_two, gradient, weight_decay):
    new_one = BETA_FIRST * moment_one + (1.0 - BETA_FIRST) * gradient
    new_two = BETA_SECOND * moment_two + (1.0 - BETA_SECOND) * gradient * gradient
    new_master = master - RATE_ADAM * (
        new_one / (jnp.sqrt(new_two) + EPS_ADAM) + weight_decay * master
    )
    return (new_master, new_one, new_two)


def shampoo_step(master, stat_left, stat_right, left_root, right_root, gradient):
    gram_left = jnp.einsum("...ij,...kj->...ik", gradient, gradient, precision=HIGH)
    gram_right = jnp.einsum("...ji,...jk->...ik", gradient, gradient, precision=HIGH)
    new_left = STAT_DECAY * stat_left + (1.0 - STAT_DECAY) * gram_left
    new_right = STAT_DECAY * stat_right + (1.0 - STAT_DECAY) * gram_right
    shaped = jnp.einsum("...ij,...jk->...ik", left_root, gradient, precision=HIGH)
    shaped = jnp.einsum("...ij,...jk->...ik", shaped, right_root, precision=HIGH)
    new_master = master - RATE_SHAMPOO * (shaped + DECAY_LAYER * master)
    return (new_master, new_left, new_right)


def product(left_side, right_side):
    return jnp.dot(left_side, right_side, preferred_element_type=jnp.float32)


def against_rows(left_side, right_side):
    return lax.dot_general(
        left_side, right_side, (((1,), (1,)), ((), ())), preferred_element_type=jnp.float32
    )


def over_rows(left_side, right_side):
    return lax.dot_general(
        left_side, right_side, (((0,), (0,)), ((), ())), preferred_element_type=jnp.float32
    )


def combine_stats(first_side, second_side):
    top_one, total_one, target_one = first_side
    top_two, total_two, target_two = second_side
    top_both = jnp.maximum(top_one, top_two)
    total_both = total_one * jnp.exp(top_one - top_both) + total_two * jnp.exp(top_two - top_both)
    return (top_both, total_both, target_one + target_two)


def local(
    input_ids,
    seq_lengths,
    loss_positions,
    targets,
    block_owner,
    layer_master,
    stats_left,
    stats_right,
    root_left,
    root_right,
    table_master,
    table_first,
    table_second,
    vector_master,
    vector_first,
    vector_second,
):
    model_ways = lax.axis_size("mp")
    data_ways = lax.axis_size("dp")
    model_rank = lax.axis_index("mp")
    inner_width = D // model_ways
    hidden = FF // model_ways
    heads_here = HEADS // model_ways
    ff_rows = FF // D
    block_count = layer_master.shape[1] * data_ways
    vocab_here = table_master.shape[0] * data_ways
    rows_micro = input_ids.shape[0] // MB
    token_count = rows_micro * LEN
    shard_rows = token_count // model_ways
    shard_start = model_rank * shard_rows
    scale_factor = HD ** (-0.5)
    split_shape = (rows_micro, LEN, heads_here, HD)
    gathered_layer, table_low = (
        lax.all_gather(layer_master[0].astype(jnp.bfloat16), "dp", axis=0, tiled=True),
        lax.all_gather(table_master.astype(jnp.bfloat16), "dp", axis=0, tiled=True),
    )
    inverse = (
        jnp.zeros((block_count,), jnp.int32)
        .at[block_owner]
        .set(jnp.arange(block_count, dtype=jnp.int32))
    )
    natural = jnp.take(gathered_layer, inverse, axis=0)
    joined_w, output_w, upward_w, downward_w = split_pieces(natural, D, inner_width, hidden, KB)
    tail_rows = vector_master[LEN:]
    rank_first = (model_rank == 0).astype(jnp.float32)
    bias_query = lax.dynamic_slice_in_dim(tail_rows[2], model_rank * inner_width, inner_width)
    bias_value = lax.dynamic_slice_in_dim(tail_rows[3], model_rank * inner_width, inner_width)
    bias_joined = jnp.concatenate([bias_query, jnp.zeros((inner_width,), jnp.float32), bias_value])
    bias_upward = lax.dynamic_slice_in_dim(
        tail_rows[7 : 7 + ff_rows].reshape(FF), model_rank * hidden, hidden
    )
    vocab_index = jnp.arange(vocab_here, dtype=jnp.int32)

    def own_rows(full_rows):
        return lax.dynamic_slice_in_dim(full_rows, shard_start, shard_rows, 0)

    def local_rows(token_ids):
        block_id = token_ids // VOC_DEV
        owned_here = block_id % model_ways == model_rank
        local_row = block_id // model_ways * VOC_DEV + token_ids % VOC_DEV
        return (jnp.where(owned_here, local_row, 0), owned_here)

    def scores_of(queries, key_vecs, same_seq):
        raw_scores = (
            jnp.einsum("rqhd,rkhd->rhqk", queries, key_vecs, preferred_element_type=jnp.float32)
            * scale_factor
        )
        return jnp.where(same_seq[:, None], raw_scores, MASK_FILL)

    def spread_row(part_sum, full_width, start_at):
        return lax.dynamic_update_slice_in_dim(
            jnp.zeros((full_width,), jnp.float32), part_sum, start_at, 0
        )

    for micro_index in range(MB):
        lower_row = micro_index * rows_micro
        upper_row = lower_row + rows_micro
        segment, offset = jax.vmap(positions_of, in_axes=(0, None))(
            seq_lengths[lower_row:upper_row], LEN
        )
        micro_local_row, micro_owned_here = local_rows(input_ids[lower_row:upper_row])
        word_part = jnp.where(
            micro_owned_here[..., None],
            jnp.take(table_low, micro_local_row, axis=0),
            jnp.zeros((), jnp.bfloat16),
        )
        word_rows = lax.psum(word_part, "mp").astype(jnp.float32)
        embedded = (word_rows + jnp.take(vector_master, offset, axis=0)).reshape(token_count, D)
        normed_x, x_normed, x_inv = norm_forward(embedded, tail_rows[0], tail_rows[1])
        x_low = normed_x.astype(jnp.bfloat16)
        joined_low = (product(x_low, joined_w) + bias_joined).astype(jnp.bfloat16)
        micro_queries = joined_low[:, :inner_width].reshape(split_shape)
        micro_key_vecs = joined_low[:, inner_width : 2 * inner_width].reshape(split_shape)
        value_vecs = joined_low[:, 2 * inner_width :].reshape(split_shape)
        micro_same_seq = segment[:, :, None] == segment[:, None, :]
        scores = scores_of(micro_queries, micro_key_vecs, micro_same_seq)
        top_score = jnp.max(scores, axis=-1, keepdims=True)
        exp_scores = jnp.exp(scores - top_score)
        denominator = jnp.sum(exp_scores, axis=-1, keepdims=True)
        log_norm = top_score + jnp.log(denominator)
        attn_low = (exp_scores / denominator).astype(jnp.bfloat16)
        mixed_low = (
            jnp.einsum("rhqk,rkhd->rqhd", attn_low, value_vecs, preferred_element_type=jnp.float32)
            .reshape(token_count, inner_width)
            .astype(jnp.bfloat16)
        )
        attended_part = (
            lax.psum_scatter(product(mixed_low, output_w), "mp", scatter_dimension=0, tiled=True)
            + tail_rows[4]
        )
        first_part, first_normed_part, first_inv_part = norm_forward(
            own_rows(normed_x) + attended_part, tail_rows[5], tail_rows[6]
        )
        first_normed = lax.all_gather(first_normed_part, "mp", axis=0, tiled=True)
        first_inv = lax.all_gather(first_inv_part, "mp", axis=0, tiled=True)
        first_out = first_normed * tail_rows[5] + tail_rows[6]
        first_low = first_out.astype(jnp.bfloat16)
        upper_pre = product(first_low, upward_w) + bias_upward
        acted_low = gelu_exact(upper_pre).astype(jnp.bfloat16)
        branch_part = (
            lax.psum_scatter(product(acted_low, downward_w), "mp", scatter_dimension=0, tiled=True)
            + tail_rows[7 + ff_rows]
        )
        second_part, second_normed_part, second_inv_part = norm_forward(
            first_part + branch_part, tail_rows[8 + ff_rows], tail_rows[9 + ff_rows]
        )
        second_normed = lax.all_gather(second_normed_part, "mp", axis=0, tiled=True)
        second_inv = lax.all_gather(second_inv_part, "mp", axis=0, tiled=True)
        second_out = second_normed * tail_rows[8 + ff_rows] + tail_rows[9 + ff_rows]
        flat_places = (
            jnp.arange(rows_micro, dtype=jnp.int32)[:, None] * LEN
            + loss_positions[lower_row:upper_row]
        ).reshape(-1)
        picked_low = jnp.take(second_out, flat_places, axis=0).astype(jnp.bfloat16)
        logits = against_rows(picked_low, table_low)
        local_top = jnp.max(logits, axis=-1)
        local_total = jnp.sum(jnp.exp(logits - local_top[:, None]), axis=-1)
        target_row, target_here = local_rows(targets[lower_row:upper_row].reshape(-1))
        target_hit = (vocab_index[None, :] == target_row[:, None]) & target_here[:, None]
        local_target = jnp.sum(jnp.where(target_hit, logits, 0.0), axis=-1)
        global_top, exp_total, target_logit = joined_2(
            (local_top, local_total, local_target), "mp", combine_stats
        )
        exp_logits = jnp.exp(logits - global_top[:, None])
        loss_part = jnp.sum(jnp.log(exp_total) + global_top - target_logit) * rank_first
        grad_logits = (exp_logits / exp_total[:, None] - target_hit.astype(jnp.float32)).astype(
            jnp.bfloat16
        )
        grad_picked = lax.psum(product(grad_logits, table_low), "mp")
        table_grad = over_rows(grad_logits, picked_low)
        grad_second = jnp.zeros((token_count, D), jnp.float32).at[flat_places].set(grad_picked)
        grad_pre2, gain_two, shift_two = norm_backward(
            grad_second, second_normed, second_inv, tail_rows[8 + ff_rows]
        )
        branch_grad = grad_pre2.astype(jnp.bfloat16)
        downward_grad = over_rows(acted_low, branch_grad)
        acted_grad = against_rows(branch_grad, downward_w)
        upper_grad = (acted_grad * gelu_slope(upper_pre)).astype(jnp.bfloat16)
        upward_grad = over_rows(first_low, upper_grad)
        grad_first = lax.psum(against_rows(upper_grad, upward_w), "mp") + grad_pre2
        grad_pre1, gain_one, shift_one = norm_backward(
            grad_first, first_normed, first_inv, tail_rows[5]
        )
        attended_grad = grad_pre1.astype(jnp.bfloat16)
        output_grad = over_rows(mixed_low, attended_grad)
        mixed_grad = against_rows(attended_grad, output_w).astype(jnp.bfloat16).reshape(split_shape)
        scores = scores_of(micro_queries, micro_key_vecs, micro_same_seq)
        attn_probs = jnp.exp(scores - log_norm)
        attn_low = attn_probs.astype(jnp.bfloat16)
        value_grad = jnp.einsum(
            "rhqk,rqhd->rkhd", attn_low, mixed_grad, preferred_element_type=jnp.float32
        )
        probs_grad = jnp.einsum(
            "rqhd,rkhd->rhqk", mixed_grad, value_vecs, preferred_element_type=jnp.float32
        )
        inner_sum = jnp.sum(probs_grad * attn_probs, axis=-1, keepdims=True)
        scores_grad = (attn_probs * (probs_grad - inner_sum)).astype(jnp.bfloat16)
        query_grad = (
            jnp.einsum(
                "rhqk,rkhd->rqhd", scores_grad, micro_key_vecs, preferred_element_type=jnp.float32
            )
            * scale_factor
        )
        key_grad = (
            jnp.einsum(
                "rhqk,rqhd->rkhd", scores_grad, micro_queries, preferred_element_type=jnp.float32
            )
            * scale_factor
        )
        joined_grad = jnp.concatenate(
            [
                query_grad.reshape(token_count, inner_width),
                key_grad.reshape(token_count, inner_width),
                value_grad.reshape(token_count, inner_width),
            ],
            axis=1,
        ).astype(jnp.bfloat16)
        joined_wgrad = over_rows(x_low, joined_grad)
        grad_x_part = lax.psum_scatter(
            against_rows(joined_grad, joined_w), "mp", scatter_dimension=0, tiled=True
        ) + own_rows(grad_pre1)
        grad_embed_part, gain_zero, shift_zero = norm_backward(
            grad_x_part, own_rows(x_normed), own_rows(x_inv), tail_rows[0]
        )
        grad_embed = lax.all_gather(grad_embed_part, "mp", axis=0, tiled=True)
        table_grad = table_grad + jax.ops.segment_sum(
            jnp.where(micro_owned_here.reshape(-1)[:, None], grad_embed, 0.0),
            micro_local_row.reshape(-1),
            num_segments=vocab_here,
        )
        position_grad = jax.ops.segment_sum(
            grad_embed_part, own_rows(offset.reshape(-1)), num_segments=LEN
        )
        joined_sums = jnp.sum(joined_grad.astype(jnp.float32), axis=0)
        zero_row = jnp.zeros((D,), jnp.float32)
        shared = (
            jnp.concatenate(
                [
                    jnp.zeros((LEN, D), jnp.float32),
                    jnp.stack(
                        [
                            zero_row,
                            zero_row,
                            zero_row,
                            zero_row,
                            jnp.sum(attended_grad.astype(jnp.float32), axis=0),
                            gain_one,
                            shift_one,
                        ]
                    ),
                    jnp.zeros((ff_rows, D), jnp.float32),
                    jnp.stack(
                        [jnp.sum(branch_grad.astype(jnp.float32), axis=0), gain_two, shift_two]
                    ),
                ],
                axis=0,
            )
            * rank_first
        )
        query_row = spread_row(joined_sums[:inner_width], D, model_rank * inner_width)
        value_row = spread_row(joined_sums[2 * inner_width :], D, model_rank * inner_width)
        upward_rows = spread_row(
            jnp.sum(upper_grad.astype(jnp.float32), axis=0), FF, model_rank * hidden
        ).reshape(ff_rows, D)
        sliced = jnp.concatenate(
            [
                position_grad,
                jnp.stack([gain_zero, shift_zero, query_row, value_row]),
                jnp.zeros((3, D), jnp.float32),
                upward_rows,
                jnp.zeros((3, D), jnp.float32),
            ],
            axis=0,
        )
        vector_grad = shared + sliced
        natural_grad = jnp.concatenate(
            [
                to_tiles(joined_wgrad, KB),
                to_tiles(output_grad, KB),
                to_tiles(upward_grad, KB),
                to_tiles(downward_grad, KB),
            ],
            axis=0,
        )
        owner_grad = jnp.take(natural_grad, block_owner, axis=0)
        owner_grad, table_grad, vector_grad, loss_part = (
            owner_grad,
            table_grad,
            vector_grad,
            loss_part,
        )
        if micro_index == 0:
            layer_total, table_total, vector_total, loss_total = (
                owner_grad,
                table_grad,
                vector_grad,
                loss_part,
            )
        else:
            layer_total = layer_total + owner_grad
            table_total = table_total + table_grad
            vector_total = vector_total + vector_grad
            loss_total = loss_total + loss_part
    layer_total, table_total = (
        lax.psum_scatter(layer_total, "dp", scatter_dimension=0, tiled=True),
        lax.psum_scatter(table_total, "dp", scatter_dimension=0, tiled=True),
    )
    shard_squares = jnp.sum(layer_total * layer_total) + jnp.sum(table_total * table_total)
    vector_sum, loss_sum, squares_sum = lax.psum(
        (vector_total, loss_total, shard_squares), ("dp", "mp")
    )
    squares = squares_sum + jnp.sum(vector_sum * vector_sum)
    grad_norm = jnp.sqrt(squares)
    count_all = input_ids.shape[0] * data_ways * POS
    limit = CLIP_FACTOR * math.sqrt(count_all)
    factor = jnp.minimum(1.0, limit / grad_norm)
    layer_new, left_new, right_new = shampoo_step(
        layer_master, stats_left, stats_right, root_left, root_right, (layer_total * factor)[None]
    )
    table_new, table_one, table_two = adam_step(
        table_master, table_first, table_second, table_total * factor, DECAY_TABLE
    )
    vector_new, vector_one, vector_two = adam_step(
        vector_master, vector_first, vector_second, vector_sum * factor, 0.0
    )
    loss = loss_sum / jnp.float32(count_all)
    return (
        loss,
        grad_norm,
        layer_new,
        left_new,
        right_new,
        table_new,
        table_one,
        table_two,
        vector_new,
        vector_one,
        vector_two,
    )


def solution(mesh):
    return jax.shard_map(
        local,
        mesh=mesh,
        in_specs=(
            P("dp", None),
            P("dp", None),
            P("dp", None),
            P("dp", None),
            P(),
            P("mp", "dp", None, None),
            P("mp", "dp", None, None),
            P("mp", "dp", None, None),
            P("mp", "dp", None, None),
            P("mp", "dp", None, None),
            P(("dp", "mp"), None),
            P(("dp", "mp"), None),
            P(("dp", "mp"), None),
            P(),
            P(),
            P(),
        ),
        out_specs=(
            P(),
            P(),
            P("mp", "dp", None, None),
            P("mp", "dp", None, None),
            P("mp", "dp", None, None),
            P(("dp", "mp"), None),
            P(("dp", "mp"), None),
            P(("dp", "mp"), None),
            P(),
            P(),
            P(),
        ),
        check_vma=False,
    )
```

profile of v0, /device:TPU:0, one launch (start us, length us, event | category | flops | bytes accessed | tf_op | source)
XLA Modules:
  0.0 1432.5 jit_solution(13816121997652633018)
XLA Ops:
  11.7 63.8 %all-gather.39.cloned.1.call-done = bf16[8,197,1024]{2,1,0:T(8,128)(2,1)} async-done(((bf16[1,197,1024]{2,1,0:T(8,128)(2,1)}), bf16[8,197,1024]{2,1,0:T(8,128)(2,1)}) %all-gather.39.cloned.1.call-update) | async-done | bytes 3227664 | tf_op jit(solution)/shard_map/all_gather | solution.py:182
  106.2 37.7 %all-reduce.24.cloned.1.call-done = (bf16[1,512,1024]{2,1,0:T(8,128)(2,1)}, bf16[1,512,1024]{2,1,0:T(8,128)(2,1)}) async-done(((bf16[1,512,1024]{2,1,0:T(8,128)(2,1)}, bf16[1,512,1024]{2,1,0:T(8,128)(2,1)}), (bf16[1,512,1024]{2,1,0:T(8,128)(2,1)}, bf16[1,512,1024]{2,1,0:T(8,128)(2,1)})) %all-reduce.24.cloned.1.call-update) | async-done | bytes 2097168 | tf_op jit(solution)/shard_map/psum | solution.py:234
  147.3 98.7 %all-gather.37.cloned.1.call-done = bf16[1,192,128,128]{3,2,0,1:T(8,128)(2,1)} async-done(((bf16[1,24,128,128]{3,2,0,1:T(8,128)(2,1)}), bf16[1,192,128,128]{3,2,0,1:T(8,128)(2,1)}) %all-gather.37.cloned.1.call-update) | async-done | bytes 6291472 | tf_op jit(solution)/shard_map/all_gather | solution.py:181
  246.0 10.8 gather_fusion
  314.0 32.9 %reduce-scatter.14.cloned.1.call-done = f32[128,1024]{1,0:T(8,128)} async-done(((f32[512,1024]{1,0:T(8,128)}), f32[128,1024]{1,0:T(8,128)}) %reduce-scatter.14.cloned.1.call-update) | async-done | bytes 524304 | tf_op jit(solution)/shard_map/reduce_scatter | solution.py:255
  361.6 11.4 all-gather.25.cloned.1.call-done
  377.8 20.0 %all-gather.29.cloned.1.call-done = f32[512,1024]{1,0:T(8,128)} async-done(((f32[128,1024]{1,0:T(8,128)}), f32[512,1024]{1,0:T(8,128)}) %all-gather.29.cloned.1.call-update) | async-done | bytes 2097168 | tf_op jit(solution)/shard_map/all_gather | solution.py:261
  412.7 26.9 %reduce-scatter.12.cloned.1.call-done = f32[128,1024]{1,0:T(8,128)} async-done(((f32[512,1024]{1,0:T(8,128)}), f32[128,1024]{1,0:T(8,128)}) %reduce-scatter.12.cloned.1.call-update) | async-done | bytes 524304 | tf_op jit(solution)/shard_map/reduce_scatter | solution.py:268
  439.6 34.0 %reduce-scatter.16.cloned.1.call-done = f32[128,1024]{1,0:T(8,128)} async-done(((f32[512,1024]{1,0:T(8,128)}), f32[128,1024]{1,0:T(8,128)}) %reduce-scatter.16.cloned.1.call-update) | async-done | bytes 524304 | tf_op jit(solution)/shard_map/reduce_scatter | solution.py:268
  480.5 19.3 %all-gather.27.cloned.1.call-done = f32[512,1024]{1,0:T(8,128)} async-done(((f32[128,1024]{1,0:T(8,128)}), f32[512,1024]{1,0:T(8,128)}) %all-gather.27.cloned.1.call-update) | async-done | bytes 2097168 | tf_op jit(solution)/shard_map/all_gather | solution.py:274
  499.8 24.8 %all-gather.31.cloned.1.call-done = f32[512,1024]{1,0:T(8,128)} async-done(((f32[128,1024]{1,0:T(8,128)}), f32[512,1024]{1,0:T(8,128)}) %all-gather.31.cloned.1.call-update) | async-done | bytes 2097168 | tf_op jit(solution)/shard_map/all_gather | solution.py:274
  543.2 10.2 all-reduce.9
  569.8 25.0 %all-reduce.22.cloned.1.call-done = (f32[80,1024]{1,0:T(8,128)}, f32[80,1024]{1,0:T(8,128)}) async-done(((f32[80,1024]{1,0:T(8,128)}, f32[80,1024]{1,0:T(8,128)}), (f32[80,1024]{1,0:T(8,128)}, f32[80,1024]{1,0:T(8,128)})) %all-reduce.22.cloned.1.call-update) | async-done | bytes 655376 | tf_op jit(solution)/shard_map/psum | solution.py:296
  628.4 79.8 %all-reduce.20.cloned.1.call-done = (f32[512,1024]{1,0:T(8,128)}, f32[512,1024]{1,0:T(8,128)}) async-done(((f32[512,1024]{1,0:T(8,128)}, f32[512,1024]{1,0:T(8,128)}), (f32[512,1024]{1,0:T(8,128)}, f32[512,1024]{1,0:T(8,128)})) %all-reduce.20.cloned.1.call-update) | async-done | bytes 4194320 | tf_op jit(solution)/shard_map/psum | solution.py:307
  744.0 13.7 reduce-scatter.20.cloned.1.call-done
  759.2 32.4 %reduce-scatter.22.cloned.1.call-done = f32[128,1024]{1,0:T(8,128)} async-done(((f32[512,1024]{1,0:T(8,128)}), f32[128,1024]{1,0:T(8,128)}) %reduce-scatter.22.cloned.1.call-update) | async-done | bytes 524304 | tf_op jit(solution)/shard_map/reduce_scatter | solution.py:346
  847.4 15.4 %gather_fusion.7 = f32[192,128,128]{2,1,0:T(8,128)} fusion(f32[192,128,128]{2,1,0:T(8,128)} %pad_maximum_fusion, s32[1024]{0:T(1024)S(1)} %pad_clamp_fusion), kind=kCustom, calls=%fused_computation.3.clone | custom fusion | bytes 25166592 | tf_op jit(solution)/shard_map/jit(_take)/gather | solution.py:412
  874.4 15.3 %gather_fusion.8 = f32[192,128,128]{2,1,0:T(8,128)} fusion(f32[192,128,128]{2,1,0:T(8,128)} %pad_maximum_fusion.1, s32[1024]{0:T(1024)S(1)} %pad_clamp_fusion), kind=kCustom, calls=%fused_computation.7.clone | custom fusion | bytes 25166592 | tf_op jit(solution)/shard_map/jit(_take)/gather | solution.py:412
  889.7 15.1 %select_add_fusion = f32[192,128,128]{2,1,0:T(8,128)} fusion(f32[192,128,128]{2,1,0:T(8,128)} %gather_fusion.8, f32[192,128,128]{2,1,0:T(8,128)} %gather_fusion.7, pred[192]{0:T(512)(128)(4,1)S(1)} %compare_and_fusion), kind=kLoop, calls=%fused_computation.37 | loop fusion | flops 9437184 | bytes 37748928 | tf_op jit(solution)/shard_map/add | solution.py:427
  972.7 15.8 %scatter_custom_fusion.3 = f32[1576,1024]{1,0:T(8,128)} fusion(f32[1576,1024]{1,0:T(8,128)} %convolution_add_fusion, s32[1024]{0:T(1024)S(1)} %bitcast.599, f32[512,1024]{1,0:T(8,128)} %broadcast_select_fusion.1, f32[]{:T(128)} %constant.327.clone.1, f32[512,1024]{1,0:T(8,128)} %broadcast_select_fusion.2), kind=kCustom, calls=%fused_computation.40 | custom fusion | flops 2097152 | bytes 10650112 | tf_op jit(solution)/shard_map/add | solution.py:428
  988.4 169.0 %fusion = f32[200,1024]{1,0:T(8,128)S(1)} fusion(f32[1576,1024]{1,0:T(8,128)} %scatter_custom_fusion.3), kind=kCustom, calls=%all-reduce-scatter | all-reduce-scatter fusion | flops 1638401 | bytes 7275008
  1167.5 45.6 %reduce-scatter.18.cloned.1.call-done = f32[24,128,128]{2,1,0:T(8,128)} async-done(((f32[192,128,128]{2,1,0:T(8,128)}), f32[24,128,128]{2,1,0:T(8,128)}) %reduce-scatter.18.cloned.1.call-update) | async-done | bytes 1572880 | tf_op jit(solution)/shard_map/reduce_scatter | solution.py:432
  1216.8 138.0 %all-reduce.18.cloned.1.call-done = f32[526,1024]{1,0:T(8,128)} async-done(((f32[526,1024]{1,0:T(8,128)}), f32[526,1024]{1,0:T(8,128)}) %all-reduce.18.cloned.1.call-update) | async-done | bytes 2154512 | tf_op jit(solution)/shard_map/psum | solution.py:436
  1357.6 39.5 %all-reduce.8 = (f32[]{:T(128)}, f32[]{:T(128)}) all-reduce(f32[]{:T(128)S(6)} %add.754, f32[]{:T(128)S(6)} %add.768), channel_id=1, replica_groups=mesh['dp'=8,'mp'=4] {'dp','mp'}, use_global_device_ids=true, to_apply=%region_41.45 | all-reduce | flops 2 | bytes 16 | tf_op jit(solution)/shard_map/psum | solution.py:436
  (522 shorter events, 413.4 us)
Async XLA Ops:
  7.2 1395.3 %copy-start = (f32[1,24,128,128]{3,2,1,0:T(8,128)S(1)}, f32[1,24,128,128]{3,2,1,0:T(8,128)}, u32[]{:S(2)}) copy-start(f32[1,24,128,128]{3,2,1,0:T(8,128)} %param.36) | copy-start | bytes 4718596
  7.2 68.3 %all-gather.39.cloned.1.call-start = ((), (), s32[]{:S(2)}) async-start(), calls=%async_computation.22 | async-start | bytes 3686400 | tf_op jit(solution)/shard_map/all_gather | solution.py:182
  9.3 134.6 %all-reduce.24.cloned.1.call-start = ((), (), s32[]{:S(2)}) async-start(), calls=%async_computation.25 | async-start | bytes 4194304 | tf_op jit(solution)/shard_map/psum | solution.py:234
  10.2 80.7 %copy-start.79 = (pred[512]{0:T(512)(128)(4,1)}, pred[512]{0:T(512)(128)(4,1)S(1)}, u32[]{:S(2)}) copy-start(pred[512]{0:T(512)(128)(4,1)S(1)} %get-tuple-element.561) | copy-start | bytes 1540
  93.5 152.5 %all-gather.37.cloned.1.call-start = ((), (), s32[]{:S(2)}) async-start(), calls=%async_computation.21 | async-start | bytes 7077888 | tf_op jit(solution)/shard_map/all_gather | solution.py:181
  95.9 218.0 %reduce-scatter.10.cloned.1.call-start = ((), (), s32[]{:S(2)}) async-start(), calls=%async_computation.7 | async-start | bytes 2621440 | tf_op jit(solution)/shard_map/reduce_scatter | solution.py:255
  282.7 64.1 %reduce-scatter.14.cloned.1.call-start = ((), (), s32[]{:S(2)}) async-start(), calls=%async_computation.11 | async-start | bytes 2621440 | tf_op jit(solution)/shard_map/reduce_scatter | solution.py:255
  307.6 65.4 %all-gather.25.cloned.1.call-start = ((), (), s32[]{:S(2)}) async-start(), calls=%async_computation.8 | async-start | bytes 2621440 | tf_op jit(solution)/shard_map/all_gather | solution.py:261
  350.3 47.6 %all-gather.29.cloned.1.call-start = ((), (), s32[]{:S(2)}) async-start(), calls=%async_computation.12 | async-start | bytes 2621440 | tf_op jit(solution)/shard_map/all_gather | solution.py:261
  352.1 87.5 %reduce-scatter.12.cloned.1.call-start = ((), (), s32[]{:S(2)}) async-start(), calls=%async_computation.9 | async-start | bytes 2621440 | tf_op jit(solution)/shard_map/reduce_scatter | solution.py:268
  408.0 65.5 %reduce-scatter.16.cloned.1.call-start = ((), (), s32[]{:S(2)}) async-start(), calls=%async_computation.13 | async-start | bytes 2621440 | tf_op jit(solution)/shard_map/reduce_scatter | solution.py:268
  412.6 87.2 %all-gather.27.cloned.1.call-start = ((), (), s32[]{:S(2)}) async-start(), calls=%async_computation.10 | async-start | bytes 2621440 | tf_op jit(solution)/shard_map/all_gather | solution.py:274
  477.1 47.6 %all-gather.31.cloned.1.call-start = ((), (), s32[]{:S(2)}) async-start(), calls=%async_computation.14 | async-start | bytes 2621440 | tf_op jit(solution)/shard_map/all_gather | solution.py:274
  478.8 116.0 %all-reduce.22.cloned.1.call-start = ((), (), s32[]{:S(2)}) async-start(), calls=%async_computation.24 | async-start | bytes 1310720 | tf_op jit(solution)/shard_map/psum | solution.py:296
  559.7 148.5 %all-reduce.20.cloned.1.call-start = ((), (), s32[]{:S(2)}) async-start(), calls=%async_computation.23 | async-start | bytes 8388608 | tf_op jit(solution)/shard_map/psum | solution.py:307
  622.3 135.3 %reduce-scatter.20.cloned.1.call-start = ((), (), s32[]{:S(2)}) async-start(), calls=%async_computation.16 | async-start | bytes 2621440 | tf_op jit(solution)/shard_map/reduce_scatter | solution.py:346
  725.9 65.7 %reduce-scatter.22.cloned.1.call-start = ((), (), s32[]{:S(2)}) async-start(), calls=%async_computation.18 | async-start | bytes 2621440 | tf_op jit(solution)/shard_map/reduce_scatter | solution.py:346
  743.7 222.1 %all-gather.35.cloned.1.call-start = ((), (), s32[]{:S(2)}) async-start(), calls=%async_computation.19 | async-start | bytes 2621440 | tf_op jit(solution)/shard_map/all_gather | solution.py:352
  796.3 173.3 %all-gather.33.cloned.1.call-start = ((), (), s32[]{:S(2)}) async-start(), calls=%async_computation.17 | async-start | bytes 2621440 | tf_op jit(solution)/shard_map/all_gather | solution.py:352
  836.1 377.1 %reduce-scatter.18.cloned.1.call-start = ((), (), s32[]{:S(2)}) async-start(), calls=%async_computation.15 | async-start | bytes 14155776 | tf_op jit(solution)/shard_map/reduce_scatter | solution.py:432
  904.9 450.0 %all-reduce.18.cloned.1.call-start = ((), (), s32[]{:S(2)}) async-start(), calls=%async_computation.20 | async-start | bytes 4325376 | tf_op jit(solution)/shard_map/psum | solution.py:436
  988.4 173.6 %copy-start.62 = (f32[80]{0:T(128)S(1)}, f32[80]{0:T(128)}, u32[]{:S(2)}) copy-start(f32[80]{0:T(128)} %copy-done.61) | copy-start | bytes 964
  1157.5 8.6 collective-permute-start
  1166.7 191.0 %copy-start.28 = (f32[221,1024]{1,0:T(8,128)}, f32[221,1024]{1,0:T(8,128)S(1)}, u32[]{:S(2)}) copy-start(f32[221,1024]{1,0:T(8,128)S(1)} %concatenate.46) | copy-start | bytes 2715652
  (103 other events, 702.3 us)
Sparse Core Ops, SparseCore 0:
  10.8 64.6 all-gather.38
  93.6 50.2 all-reduce.23
  146.9 99.0 all-gather.36
  282.8 29.6 reduce-scatter.9
  315.4 31.3 reduce-scatter.13
  350.4 22.5 all-gather.24
  375.2 22.5 all-gather.28
  408.1 31.3 reduce-scatter.11
  442.1 31.4 reduce-scatter.15
  477.2 22.5 all-gather.26
  502.0 22.5 all-gather.30
  559.8 34.9 all-reduce.21
  622.4 85.6 all-reduce.19
  726.1 31.5 reduce-scatter.19
  760.2 31.3 reduce-scatter.21
  796.4 22.5 all-gather.34
  836.2 22.6 all-gather.32
  905.0 308.0 reduce-scatter.17
  1219.3 135.5 all-reduce.17
where the time goes:
time: 1440 us; the launch traced here: 1430 us
  waiting for transfers between devices  707 us (49%)
  blocking collectives  239 us (17%)
  local copies, waits for them, and re-layouts  193 us (13%)
  other arithmetic  157 us (11%)
  matrix products  105 us (7%)
  between operations  24.1 us (2%)
    unnamed x2, blocking collectives  179 us
    psum x1, waiting for transfers between devices, local(): lax.psum((vector_total, loss_total, shard_squares), ('dp', 'mp'))  138 us
    all_gather x1, waiting for transfers between devices, local(): lax.all_gather(layer_master[0].astype(jnp.bfloat16), 'dp', axis=0, tiled=...  98.7 us
    psum x1, waiting for transfers between devices, local(): grad_first = lax.psum(against_rows(upper_grad, upward_w), 'mp') + grad_pre2  79.8 us
    all_gather x1, waiting for transfers between devices, local(): lax.all_gather(table_master.astype(jnp.bfloat16), 'dp', axis=0, tiled=True)  63.8 us
    reduce_scatter x2, waiting for transfers between devices, local(): lax.psum_scatter(product(acted_low, downward_w), 'mp', scatter_dimension=...  60.9 us
    reduce_scatter x2, waiting for transfers between devices, local(): lax.psum_scatter(against_rows(joined_grad, joined_w), 'mp', scatter_dimen...  46 us
    reduce_scatter x1, waiting for transfers between devices, local(): lax.psum_scatter(layer_total, 'dp', scatter_dimension=0, tiled=True)  45.6 us
  transfers between devices with their start and end apart: 20, of which 17 were waited for; matrix products, arithmetic and copies ran while one was open for 31% of the time, Pallas kernels for 0%

commit v1 on v0

v1 whole, which is shorter than its diff:
```python
import math

import jax
import jax.numpy as jnp
from jax import lax
from jax.experimental import pallas as pl
from jax.experimental.pallas import tpu as pltpu
from jax.sharding import PartitionSpec as P

D = 1024
HEADS = 16
HD = 64
FF = 4096
VOC_DEV = 197
VOC_PAD = 208
LEN = 512
POS = 80
KB = 128

HIGH = lax.Precision.HIGHEST
EPS_NORM = 1e-05
EPS_ADAM = 1e-08
BETA_FIRST = 0.5
BETA_SECOND = 0.5
RATE_ADAM = 0.01
RATE_SHAMPOO = 0.03
DECAY_TABLE = 0.01
DECAY_LAYER = 0.01
STAT_DECAY = 0.5
CLIP_FACTOR = 16.0
MASK_FILL = -1000000000.0
RING = 4
VMEM_LIMIT = 56 * 1024 * 1024

f32 = jnp.float32
bf16 = jnp.bfloat16
f16 = jnp.float16


def swap(value, axis, ways, bit):
    pairs = [(i, i ^ bit) for i in range(ways)]
    return jax.tree.map(lambda part: lax.ppermute(part, axis, pairs), value)


def ring_step(value):
    pairs = [(i, (i + 2) % (2 * RING)) for i in range(2 * RING)]
    return lax.ppermute(value, "dp", pairs)


def after(values, *others):
    flat, tree = jax.tree.flatten(values)
    tied = lax.optimization_barrier(tuple(flat) + tuple(others))
    return jax.tree.unflatten(tree, tied[: len(flat)])


def gather_stream(parts):
    held = [[part] for part in parts]
    crossed = [[] for _ in parts]
    jobs_z = [(p, k) for p in range(len(parts)) for k in range(RING - 1)]
    jobs_x = [(p, k) for p in range(len(parts)) for k in range(RING)]
    done_z = 0
    waits = ()
    for slot, (p, k) in enumerate(jobs_x):
        fresh = []
        x_source = held[p][k]
        x_source = after(x_source, *waits) if waits else x_source
        got_x = swap(x_source, "dp", 2 * RING, 1)
        fresh.append(got_x)
        if done_z < len(jobs_z):
            q, j = jobs_z[done_z]
            if len(held[q]) == j + 1:
                z_source = held[q][j]
                z_source = after(z_source, *waits) if waits else z_source
                got_z = ring_step(z_source)
                fresh.append(got_z)
                done_z += 1
                fresh = list(lax.optimization_barrier(tuple(fresh)))
                held[q].append(fresh[1])
        crossed[p].append(fresh[0])
        waits = tuple(fresh)
    return [
        [piece for k in range(RING) for piece in (held[p][k], crossed[p][k])]
        for p in range(len(parts))
    ]


def reduce_stream(stacked, kind):
    def narrow(value):
        return value.astype(kind)

    moving = None
    for slot in range(RING):
        k = (slot + 1) % RING
        outgoing = narrow(stacked[2 * k + 1])
        if moving is not None:
            outgoing, moving = lax.optimization_barrier((outgoing, moving))
        got = swap(outgoing, "dp", 2 * RING, 1)
        total = stacked[2 * k].astype(f32)
        if moving is not None:
            came = ring_step(moving)
            got, came = lax.optimization_barrier((got, came))
            total = total + came.astype(f32)
        total = total + got.astype(f32)
        moving = narrow(total)
    return total


def reduce_mp(value, ways):
    if ways != 4:
        return lax.psum(value, "mp")
    half = value.shape[0] // 2
    low_bit = lax.axis_index("mp") & 1
    mine = lax.dynamic_slice_in_dim(value, low_bit * half, half, 0)
    other = lax.dynamic_slice_in_dim(value, (1 - low_bit) * half, half, 0)
    mine = mine + swap(other, "mp", ways, 1)
    mine = mine + swap(mine, "mp", ways, 2)
    other = swap(mine, "mp", ways, 1)
    return jnp.where(
        low_bit == 0,
        jnp.concatenate([mine, other], axis=0),
        jnp.concatenate([other, mine], axis=0),
    )


def butterfly(value, combine, dp, mp, both=True):
    axes = [("mp", mp)] + ([("dp", dp)] if both else [])
    for axis, ways in axes:
        bit = 1
        while bit < ways:
            value = combine(value, swap(value, axis, ways, bit))
            bit *= 2
    return value


def gelu_exact(values):
    return 0.5 * values * (1.0 + lax.erf(values * 0.7071067811865476))


def gelu_slope(values):
    cumulative = 0.5 * (1.0 + lax.erf(values * 0.7071067811865476))
    density = jnp.exp(-0.5 * values * values) * 0.3989422804014327
    return cumulative + values * density


def norm_forward(values, norm_gain, norm_shift):
    row_mean = jnp.mean(values, axis=-1, keepdims=True)
    centered = values - row_mean
    variance = jnp.mean(centered * centered, axis=-1, keepdims=True)
    inv_dev = lax.rsqrt(variance + EPS_NORM)
    normed = centered * inv_dev
    return (normed * norm_gain + norm_shift, normed, inv_dev)


def norm_backward(grad_out, normed, inv_dev, norm_gain):
    scaled = grad_out * norm_gain
    grad_in = inv_dev * (
        scaled
        - jnp.mean(scaled, axis=-1, keepdims=True)
        - normed * jnp.mean(scaled * normed, axis=-1, keepdims=True)
    )
    return (grad_in, jnp.sum(grad_out * normed, axis=0), jnp.sum(grad_out, axis=0))


def positions_of(lengths):
    ends = jnp.stack([jnp.sum(lengths[:, : s + 1], axis=1) for s in range(lengths.shape[1])], axis=1)
    places = jnp.arange(LEN, dtype=jnp.int32)
    passed = places[None, :, None] >= ends[:, None, :]
    segment = jnp.sum(passed.astype(jnp.int32), axis=2)
    start = jnp.max(jnp.where(passed, ends[:, None, :], 0), axis=2)
    return (segment, places[None, :] - start)


def adam_step(master, moment_one, moment_two, gradient, weight_decay):
    new_one = BETA_FIRST * moment_one + (1.0 - BETA_FIRST) * gradient
    new_two = BETA_SECOND * moment_two + (1.0 - BETA_SECOND) * gradient * gradient
    new_master = master - RATE_ADAM * (
        new_one / (jnp.sqrt(new_two) + EPS_ADAM) + weight_decay * master
    )
    return (new_master, new_one, new_two)


def product(left_side, right_side):
    return jnp.dot(left_side, right_side, preferred_element_type=f32)


def against_rows(left_side, right_side):
    return lax.dot_general(
        left_side, right_side, (((1,), (1,)), ((), ())), preferred_element_type=f32
    )


def over_rows(left_side, right_side):
    return lax.dot_general(
        left_side, right_side, (((0,), (0,)), ((), ())), preferred_element_type=f32
    )


def hit_matrix(codes, count, kind=bf16):
    return (codes[:, None] == jnp.arange(count, dtype=jnp.int32)[None, :]).astype(kind)


def over_rows_exact(hits, values):
    upper = values.astype(bf16)
    rest = values - upper.astype(f32)
    lower = rest.astype(bf16)
    return over_rows(hits, upper) + over_rows(hits, lower)


def power_scale(bound):
    safe = jnp.clip(bound, 1e-30, 1e38)
    return jnp.exp2(jnp.ceil(jnp.log2(safe)) - 14.0)


def whole(count):
    return [pl.BlockSpec(memory_space=pltpu.VMEM) for _ in range(count)]


TILES = ((8, 6), (2, 8), (8, 8), (8, 8))


def unpack_kernel(slots, stacked, *outs):
    block = 0
    for (high, wide), out in zip(TILES, outs):
        for i in range(high):
            for j in range(wide):
                out[i * KB : (i + 1) * KB, j * KB : (j + 1) * KB] = stacked[slots[block]]
                block += 1


def pack_kernel(slots, *refs):
    out = refs[-1]
    block = 0
    for (high, wide), grad in zip(TILES, refs[:-1]):
        for i in range(high):
            for j in range(wide):
                tile = grad[i * KB : (i + 1) * KB, j * KB : (j + 1) * KB]
                out[slots[block]] = tile.astype(out.dtype)
                block += 1


def unpack(slots, stacked):
    return pl.pallas_call(
        unpack_kernel,
        out_shape=[jax.ShapeDtypeStruct((h * KB, w * KB), bf16) for h, w in TILES],
        in_specs=[pl.BlockSpec(memory_space=pltpu.SMEM)] + whole(1),
        out_specs=whole(4),
        compiler_params=pltpu.CompilerParams(vmem_limit_bytes=VMEM_LIMIT),
        name="unpack_weights",
    )(slots, stacked)


def pack(slots, grads, kind):
    return pl.pallas_call(
        pack_kernel,
        out_shape=jax.ShapeDtypeStruct((slots.shape[0], KB, KB), kind),
        in_specs=[pl.BlockSpec(memory_space=pltpu.SMEM)] + whole(4),
        out_specs=pl.BlockSpec(memory_space=pltpu.VMEM),
        compiler_params=pltpu.CompilerParams(vmem_limit_bytes=VMEM_LIMIT),
        name="pack_gradients",
    )(slots, *grads)


def local(
    input_ids,
    seq_lengths,
    loss_positions,
    targets,
    block_owner,
    layer_master,
    stats_left,
    stats_right,
    root_left,
    root_right,
    table_master,
    table_first,
    table_second,
    vector_master,
    vector_first,
    vector_second,
):
    mp = lax.axis_size("mp")
    dp = lax.axis_size("dp")
    fast = dp == 2 * RING
    model_rank = lax.axis_index("mp")
    data_rank = lax.axis_index("dp")
    inner = D // mp
    heads_here = HEADS // mp
    ff_rows = FF // D
    hidden = FF // mp
    rows = input_ids.shape[0]
    tokens = rows * LEN
    share = tokens // mp
    own_blocks = layer_master.shape[1]
    blocks = own_blocks * dp
    scale_factor = HD ** (-0.5)

    if fast:
        z_here, x_here = data_rank // 2, data_rank % 2

        def place_of(owner):
            return 2 * ((z_here - owner // 2) % RING) + (owner % 2 + x_here) % 2
    else:

        def place_of(owner):
            return owner

    share_start = ((model_rank % 2) * (mp // 2) + model_rank // 2) * share

    table_low = jnp.pad(table_master.astype(bf16), ((0, VOC_PAD - VOC_DEV), (0, 0)))
    layer_low = layer_master[0].astype(bf16)
    if fast:
        cut_t, cut_b = 112, own_blocks // 2
        streams = [
            gather_stream([table_low[:cut_t], layer_low[:cut_b]]),
            gather_stream([table_low[cut_t:], layer_low[cut_b:]]),
        ]
        table_all = jnp.stack(
            [jnp.concatenate([a, b], axis=0) for a, b in zip(streams[0][0], streams[1][0])]
        ).reshape(dp * VOC_PAD, D)
        layer_all = jnp.stack(
            [jnp.concatenate([a, b], axis=0) for a, b in zip(streams[0][1], streams[1][1])]
        ).reshape(blocks, KB, KB)
    else:
        table_all = lax.all_gather(table_low, "dp", axis=0, tiled=True)
        layer_all = lax.all_gather(layer_low, "dp", axis=0, tiled=True)
    vocab = dp * VOC_PAD

    natural = jnp.arange(blocks, dtype=jnp.int32)
    slot_of = jnp.sum(
        jnp.where(block_owner[None, :] == natural[:, None], natural[None, :], 0), axis=1
    )
    slots = place_of(slot_of // own_blocks) * own_blocks + slot_of % own_blocks

    def codes_of(ids):
        part = ids // VOC_DEV
        code = place_of(part // mp) * VOC_PAD + ids % VOC_DEV
        return jnp.where(part % mp == model_rank, code, -1)

    tail = vector_master[LEN:]
    rank_first = (model_rank == 0).astype(f32)
    bias_query = lax.dynamic_slice_in_dim(tail[2], model_rank * inner, inner)
    bias_value = lax.dynamic_slice_in_dim(tail[3], model_rank * inner, inner)
    bias_up = lax.dynamic_slice_in_dim(tail[7 : 7 + ff_rows].reshape(FF), model_rank * hidden, hidden)

    segment, offset = positions_of(seq_lengths)
    codes = codes_of(input_ids.reshape(-1))
    word_hits = hit_matrix(codes, vocab)
    words = reduce_mp(product(word_hits, table_all).astype(bf16), mp).astype(f32)
    places = jnp.take(vector_master[:LEN], offset.reshape(-1), axis=0)
    x_out, x_normed, x_inv = norm_forward(words + places, tail[0], tail[1])
    x_low = x_out.astype(bf16)
    flat = (jnp.arange(rows, dtype=jnp.int32)[:, None] * LEN + loss_positions).reshape(-1)
    pick_hits = hit_matrix(loss_positions.reshape(-1), LEN).reshape(rows, POS, LEN)
    picked_x = jnp.take(x_out, flat, axis=0)
    picked_x_low = picked_x.astype(bf16)
    pick_segment = jnp.take_along_axis(segment, loss_positions, axis=1)

    joined_w, output_w, upward_w, downward_w = unpack(slots, layer_all)
    query_w = joined_w[:, :inner]
    keyval_w = joined_w[:, inner:]

    keyval = product(x_low, keyval_w)
    keys_low = keyval[:, :inner].astype(bf16).reshape(rows, LEN, heads_here, HD)
    values_low = (keyval[:, inner:] + bias_value).astype(bf16).reshape(rows, LEN, heads_here, HD)
    queries_low = (product(picked_x_low, query_w) + bias_query).astype(bf16)
    queries_low = queries_low.reshape(rows, POS, heads_here, HD)
    scores = jnp.einsum("rqhd,rkhd->rhqk", queries_low, keys_low, preferred_element_type=f32)
    same = pick_segment[:, :, None] == segment[:, None, :]
    scores = jnp.where(same[:, None], scores * scale_factor, MASK_FILL)
    top = jnp.max(scores, axis=-1, keepdims=True)
    raised = jnp.exp(scores - top)
    probs = raised / jnp.sum(raised, axis=-1, keepdims=True)
    probs_low = probs.astype(bf16)
    mixed_low = (
        jnp.einsum("rhqk,rkhd->rqhd", probs_low, values_low, preferred_element_type=f32)
        .reshape(rows * POS, inner)
        .astype(bf16)
    )
    attended = reduce_mp(product(mixed_low, output_w), mp) + tail[4]
    first_out, first_normed, first_inv = norm_forward(picked_x + attended, tail[5], tail[6])
    first_low = first_out.astype(bf16)
    upper_pre = product(first_low, upward_w) + bias_up
    acted_low = gelu_exact(upper_pre).astype(bf16)
    branch = reduce_mp(product(acted_low, downward_w), mp) + tail[7 + ff_rows]
    second_out, second_normed, second_inv = norm_forward(
        first_out + branch, tail[8 + ff_rows], tail[9 + ff_rows]
    )
    picked_low = second_out.astype(bf16)

    logits = against_rows(picked_low, table_all)
    column = jnp.arange(vocab, dtype=jnp.int32)
    logits = jnp.where(column[None, :] % VOC_PAD < VOC_DEV, logits, -jnp.inf)
    target_hit = codes_of(targets.reshape(-1))[:, None] == column[None, :]
    local_top = jnp.max(logits, axis=-1)
    local_total = jnp.sum(jnp.exp(logits - local_top[:, None]), axis=-1)
    local_target = jnp.sum(jnp.where(target_hit, logits, 0.0), axis=-1)

    def join(one, two):
        high = jnp.maximum(one[0], two[0])
        total = one[1] * jnp.exp(one[0] - high) + two[1] * jnp.exp(two[0] - high)
        return jnp.stack([high, total, one[2] + two[2]])

    stats = butterfly(
        jnp.stack([local_top, local_total, local_target]), join, dp, mp, both=False
    )
    global_top, exp_total, target_logit = stats[0], stats[1], stats[2]
    loss_part = jnp.sum(jnp.log(exp_total) + global_top - target_logit) * rank_first
    grad_logits = (
        jnp.exp(logits - global_top[:, None]) / exp_total[:, None] - target_hit.astype(f32)
    ).astype(bf16)
    grad_second = reduce_mp(product(grad_logits, table_all), mp)

    grad_pre2, gain_two, shift_two = norm_backward(
        grad_second, second_normed, second_inv, tail[8 + ff_rows]
    )
    branch_grad = grad_pre2.astype(bf16)
    upper_grad = (against_rows(branch_grad, downward_w) * gelu_slope(upper_pre)).astype(bf16)
    grad_first = reduce_mp(against_rows(upper_grad, upward_w), mp) + grad_pre2
    downward_grad = over_rows(acted_low, branch_grad)
    upward_grad = over_rows(first_low, upper_grad)
    grad_pre1, gain_one, shift_one = norm_backward(grad_first, first_normed, first_inv, tail[5])
    attended_grad = grad_pre1.astype(bf16)
    output_grad = over_rows(mixed_low, attended_grad)
    mixed_grad = against_rows(attended_grad, output_w).astype(bf16)
    mixed_grad = mixed_grad.reshape(rows, POS, heads_here, HD)
    value_grad = jnp.einsum("rhqk,rqhd->rkhd", probs_low, mixed_grad, preferred_element_type=f32)
    probs_grad = jnp.einsum("rqhd,rkhd->rhqk", mixed_grad, values_low, preferred_element_type=f32)
    inner_sum = jnp.sum(probs_grad * probs, axis=-1, keepdims=True)
    scores_grad = (probs * (probs_grad - inner_sum)).astype(bf16)
    query_grad = scale_factor * jnp.einsum(
        "rhqk,rkhd->rqhd", scores_grad, keys_low, preferred_element_type=f32
    )
    key_grad = scale_factor * jnp.einsum(
        "rhqk,rqhd->rkhd", scores_grad, queries_low, preferred_element_type=f32
    )
    query_grad = query_grad.reshape(rows * POS, inner).astype(bf16)
    keyval_grad = jnp.concatenate(
        [key_grad.reshape(tokens, inner), value_grad.reshape(tokens, inner)], axis=1
    ).astype(bf16)
    joined_grad = jnp.concatenate(
        [over_rows(picked_x_low, query_grad), over_rows(x_low, keyval_grad)], axis=1
    )

    kind = bf16
    layer_grad = pack(slots, (joined_grad, output_grad, upward_grad, downward_grad), f32)
    if fast:
        layer_grad = layer_grad.reshape(dp, own_blocks, KB, KB)
        layer_total = jnp.concatenate(
            [
                reduce_stream([layer_grad[r, :cut_b] for r in range(dp)], kind),
                reduce_stream([layer_grad[r, cut_b:] for r in range(dp)], kind),
            ],
            axis=0,
        )
    else:
        layer_total = lax.psum_scatter(layer_grad, "dp", scatter_dimension=0, tiled=True)

    grad_x = against_rows(keyval_grad, keyval_w)
    pick_grad = against_rows(query_grad, query_w) + grad_pre1 * rank_first
    grad_x = grad_x + over_rows_exact(hit_matrix(flat, tokens), pick_grad)
    if mp == 4:
        half, low_bit, high_bit = tokens // 2, model_rank % 2, model_rank // 2
        mine = lax.dynamic_slice_in_dim(grad_x, low_bit * half, half, 0)
        other = lax.dynamic_slice_in_dim(grad_x, (1 - low_bit) * half, half, 0)
        mine = mine + swap(other, "mp", mp, 1)
        keep = lax.dynamic_slice_in_dim(mine, high_bit * share, share, 0)
        other = lax.dynamic_slice_in_dim(mine, (1 - high_bit) * share, share, 0)
        grad_x = keep + swap(other, "mp", mp, 2)
    else:
        grad_x = lax.dynamic_slice_in_dim(lax.psum(grad_x, "mp"), share_start, share, 0)
    grad_embed, gain_zero, shift_zero = norm_backward(
        grad_x,
        lax.dynamic_slice_in_dim(x_normed, share_start, share, 0),
        lax.dynamic_slice_in_dim(x_inv, share_start, share, 0),
        tail[0],
    )
    scale_here = power_scale(jnp.max(jnp.abs(grad_embed)))
    sent = (grad_embed / scale_here).astype(f16)
    if mp == 4:
        pair = (sent, jnp.broadcast_to(scale_here, (1, 128)))
        far = swap(pair, "mp", mp, 2)

        def wide(one):
            return one[0].astype(f32) * one[1][0, 0]

        def ordered(one, two, bit):
            return jnp.where(
                bit == 0, jnp.concatenate([one, two], 0), jnp.concatenate([two, one], 0)
            )

        halves = ordered(sent, far[0], high_bit)
        scales = ordered(pair[1], far[1], high_bit)
        near = swap((halves, scales), "mp", mp, 1)
        all_sent = ordered(halves, near[0], low_bit)
        all_scales = ordered(scales, near[1], low_bit)
        embed_all = (
            all_sent.astype(f32).reshape(mp, share, D) * all_scales[:, :1, None]
        ).reshape(tokens, D)
    else:
        embed_all = jnp.zeros((tokens, D), f32)
        embed_all = lax.psum(
            lax.dynamic_update_slice_in_dim(embed_all, grad_embed, share_start, 0), "mp"
        )

    place_rows = LEN // mp
    per_owner = place_rows // dp
    place_codes = offset.reshape(-1) - model_rank * place_rows
    place_codes = jnp.where(
        (place_codes >= 0) & (place_codes < place_rows),
        place_of(place_codes // per_owner) * per_owner + place_codes % per_owner,
        -1,
    )
    place_grad = over_rows_exact(hit_matrix(place_codes, place_rows), embed_all)
    table_grad = over_rows_exact(word_hits, embed_all) + over_rows(grad_logits, picked_low)
    if fast:
        place_parts = place_grad.reshape(dp, per_owner, D)
        both = jnp.concatenate([table_grad.reshape(dp, VOC_PAD, D), place_parts], axis=1)
        bound = jnp.max(jnp.abs(both))
        bound = butterfly(jnp.broadcast_to(bound, (1, 128)), jnp.maximum, dp, mp)[0, 0]
        scale_all = power_scale(bound * dp)
        both = both / scale_all
        cut = (VOC_PAD + per_owner) // 2
        total = scale_all * jnp.concatenate(
            [
                reduce_stream([both[r, :cut] for r in range(dp)], f16),
                reduce_stream([both[r, cut:] for r in range(dp)], f16),
            ],
            axis=0,
        )
        table_total, place_total = total[:VOC_DEV], total[VOC_PAD:]
    else:
        table_total = lax.psum_scatter(table_grad, "dp", scatter_dimension=0, tiled=True)[:VOC_DEV]
        place_total = lax.psum_scatter(place_grad, "dp", scatter_dimension=0, tiled=True)
    place_sum = lax.all_gather(
        lax.all_gather(place_total, "dp", axis=0, tiled=True), "mp", axis=0, tiled=True
    )

    def spread(part, width, start):
        return lax.dynamic_update_slice_in_dim(jnp.zeros((width,), f32), part, start, 0)

    keyval_sums = jnp.sum(keyval_grad[:, inner:].astype(f32), axis=0)
    query_sums = jnp.sum(query_grad.astype(f32), axis=0)
    up_rows = spread(jnp.sum(upper_grad.astype(f32), axis=0), FF, model_rank * hidden)
    vector_part = jnp.concatenate(
        [
            jnp.stack(
                [
                    gain_zero,
                    shift_zero,
                    spread(query_sums, D, model_rank * inner),
                    spread(keyval_sums, D, model_rank * inner),
                    jnp.sum(attended_grad.astype(f32), axis=0) * rank_first,
                    gain_one * rank_first,
                    shift_one * rank_first,
                ]
            ),
            up_rows.reshape(ff_rows, D),
            jnp.stack(
                [
                    jnp.sum(branch_grad.astype(f32), axis=0) * rank_first,
                    gain_two * rank_first,
                    shift_two * rank_first,
                    jnp.broadcast_to(loss_part, (D,)),
                ]
            ),
        ],
        axis=0,
    )
    vector_part = butterfly(vector_part, jnp.add, dp, mp)
    tail_sum, loss_sum = vector_part[:-1], vector_part[-1, 0]

    squares = (
        jnp.sum(layer_total * layer_total)
        + jnp.sum(table_total * table_total)
        + jnp.sum(place_total * place_total)
    )
    squares = butterfly(jnp.broadcast_to(squares, (1, 128)), jnp.add, dp, mp)[0, 0]
    squares = squares + jnp.sum(tail_sum * tail_sum)
    grad_norm = jnp.sqrt(squares)
    count_all = rows * dp * POS
    limit = CLIP_FACTOR * math.sqrt(count_all)
    factor = jnp.minimum(1.0, limit / grad_norm)

    gradient = layer_total[None] * factor
    gram_left = jnp.einsum("...ij,...kj->...ik", gradient, gradient, precision=HIGH)
    gram_right = jnp.einsum("...ji,...jk->...ik", gradient, gradient, precision=HIGH)
    left_new = STAT_DECAY * stats_left + (1.0 - STAT_DECAY) * gram_left
    right_new = STAT_DECAY * stats_right + (1.0 - STAT_DECAY) * gram_right
    shaped = jnp.einsum("...ij,...jk->...ik", root_left, gradient, precision=HIGH)
    shaped = jnp.einsum("...ij,...jk->...ik", shaped, root_right, precision=HIGH)
    layer_new = layer_master - RATE_SHAMPOO * (shaped + DECAY_LAYER * layer_master)

    table_new, table_one, table_two = adam_step(
        table_master, table_first, table_second, table_total * factor, DECAY_TABLE
    )
    vector_sum = jnp.concatenate([place_sum, tail_sum], axis=0)
    vector_new, vector_one, vector_two = adam_step(
        vector_master, vector_first, vector_second, vector_sum * factor, 0.0
    )
    loss = loss_sum / f32(count_all)
    return (
        loss,
        grad_norm,
        layer_new,
        left_new,
        right_new,
        table_new,
        table_one,
        table_two,
        vector_new,
        vector_one,
        vector_two,
    )


def solution(mesh):
    blocks = P("mp", "dp", None, None)
    vocab = P(("dp", "mp"), None)
    rows = P("dp", None)
    return jax.shard_map(
        local,
        mesh=mesh,
        in_specs=(rows,) * 4 + (P(),) + (blocks,) * 5 + (vocab,) * 3 + (P(),) * 3,
        out_specs=(P(), P()) + (blocks,) * 3 + (vocab,) * 3 + (P(),) * 3,
        check_vma=False,
    )
```

time: 1440 us -> 640 us (0.44)
  waiting for transfers between devices: 707 us -> 207 us
  blocking collectives: 239 us -> 33.4 us
  local copies, waits for them, and re-layouts: 193 us -> 70.8 us
  starting transfers between devices: 6.55 us -> 76.2 us
  other arithmetic: 157 us -> 115 us
  Pallas kernels: 0 us -> 17.3 us
  matrix products: 105 us -> 89.2 us
    psum x4 -> x0, waiting for transfers between devices: 281 us -> none  [the longest x1 138 us: local(): lax.psum((vector_total, loss_total, shard_squares), ('dp', 'mp'))]
    all_gather x8 -> x1, waiting for transfers between devices: 238 us -> 0.01 us  [local(): lax.all_gather(lax.all_gather(place_total, 'dp', axis=0, tiled=True), 'mp...]
    ppermute x0 -> x94, waiting for transfers between devices: none -> 207 us  [the longest x70 157 us: swap(): return jax.tree.map(lambda part: lax.ppermute(part, axis, pairs), value)]
    reduce_scatter x7 -> x0, waiting for transfers between devices: 185 us -> none  [the longest x2 60.9 us: local(): lax.psum_scatter(product(acted_low, downward_w), 'mp', scatter_dimension=...]
    unnamed x2 -> x0, blocking collectives: 179 us -> none
    ppermute x0 -> x94, starting transfers between devices: none -> 76.2 us  [the longest x70 61.7 us: swap(): return jax.tree.map(lambda part: lax.ppermute(part, axis, pairs), value)]
    gather x9 -> x5, local copies, waits for them, and re-layouts: 67.5 us -> 13.7 us  [the longest x1 8.05 us: local(): places = jnp.take(vector_master[:LEN], offset.reshape(-1), axis=0)]
    psum x1 -> x0, blocking collectives: 39.5 us -> none  [local(): lax.psum((vector_total, loss_total, shard_squares), ('dp', 'mp'))]
  transfers between devices with their start and end apart: 20 -> 95, of which waited for: 17 -> 61; matrix products, arithmetic and copies ran while one was open for 31% -> 25% of each run, Pallas kernels for 0% -> 3%
where the time goes in v1:
time: 640 us; the launch traced here: 633 us
  waiting for transfers between devices  207 us (32%)
  other arithmetic  115 us (18%)
  matrix products  89.2 us (14%)
  starting transfers between devices  76.2 us (12%)
  local copies, waits for them, and re-layouts  70.8 us (11%)
  blocking collectives  33.4 us (5%)
  between operations  23.3 us (4%)
  Pallas kernels  17.3 us (3%)
    ppermute x70, waiting for transfers between devices, swap(): return jax.tree.map(lambda part: lax.ppermute(part, axis, pairs), value)  157 us
    ppermute x70, starting transfers between devices, swap(): return jax.tree.map(lambda part: lax.ppermute(part, axis, pairs), value)  61.7 us
    ppermute x24, waiting for transfers between devices, ring_step(): return lax.ppermute(value, 'dp', pairs)  50.3 us
    dot_general x12, matrix products, over_rows(): lax.dot_general(left_side, right_side, (((0,), (0,)), ((), ())), preferre...  39.2 us
    all_gather x1, blocking collectives, local(): lax.all_gather(place_total, 'dp', axis=0, tiled=True)  33.4 us
    unnamed x16, other arithmetic  20.7 us
    dot_general x7, matrix products, product(): return jnp.dot(left_side, right_side, preferred_element_type=f32)  15 us
    another operation x2, other arithmetic  14.5 us
  transfers between devices with their start and end apart: 95, of which 61 were waited for; matrix products, arithmetic and copies ran while one was open for 25% of the time, Pallas kernels for 3%

profile of v1, /device:TPU:0, one launch (start us, length us, event | category | flops | bytes accessed | tf_op | source)
XLA Modules:
  0.0 632.6 jit_solution(15529839580281307479)
XLA Ops:
  65.3 6.3 fusion.15
  84.5 11.3 %collective-permute-done.22 = bf16[12,128,128]{2,1,0:T(8,128)(2,1)} collective-permute-done((bf16[12,128,128]{2,1,0:T(8,128)(2,1)}, bf16[12,128,128]{2,1,0:T(8,128)(2,1)}, u32[]{:S(2)}, u32[]{:S(2)}) %collective-permute-start.22) | collective-permute-done | bytes 393248 | tf_op jit(solution)/shard_map/ppermute | solution.py:47
  96.3 7.8 %collective-permute-done.20 = bf16[12,128,128]{2,1,0:T(8,128)(2,1)} collective-permute-done((bf16[12,128,128]{2,1,0:T(8,128)(2,1)}, bf16[12,128,128]{2,1,0:T(8,128)(2,1)}, u32[]{:S(2)}, u32[]{:S(2)}) %collective-permute-start.20) | collective-permute-done | bytes 393248 | tf_op jit(solution)/shard_map/ppermute | solution.py:47
  109.7 8.0 %gather_fusion = f32[1024,1024]{1,0:T(8,128)} fusion(f32[512,1024]{1,0:T(8,128)} %slice.256, s32[1024]{0:T(1024)S(1)} %broadcast_clamp_fusion), kind=kCustom, calls=%fused_computation | custom fusion | bytes 8392704 | tf_op jit(solution)/shard_map/jit(_take)/gather | solution.py:349
  132.0 6.9 %collective-permute-done.27 = bf16[12,128,128]{2,1,0:T(8,128)(2,1)S(1)} collective-permute-done((bf16[12,128,128]{2,1,0:T(8,128)(2,1)}, bf16[12,128,128]{2,1,0:T(8,128)(2,1)S(1)}, u32[]{:S(2)}, u32[]{:S(2)}) %collective-permute-start.27) | collective-permute-done | bytes 393248 | tf_op jit(solution)/shard_map/ppermute | solution.py:42
  147.4 8.0 %collective-permute-done.29 = bf16[12,128,128]{2,1,0:T(8,128)(2,1)S(1)} collective-permute-done((bf16[12,128,128]{2,1,0:T(8,128)(2,1)}, bf16[12,128,128]{2,1,0:T(8,128)(2,1)S(1)}, u32[]{:S(2)}, u32[]{:S(2)}) %collective-permute-start.29) | collective-permute-done | bytes 393248 | tf_op jit(solution)/shard_map/ppermute | solution.py:42
  156.3 7.2 %unpack_weights.1 = (bf16[1024,768]{1,0:T(8,128)(2,1)}, bf16[256,1024]{1,0:T(8,128)(2,1)}, bf16[1024,1024]{1,0:T(8,128)(2,1)}, bf16[1024,1024]{1,0:T(8,128)(2,1)}) custom-call(s32[192]{0:T(256)} %fusion.165.slots, bf16[192,128,128]{2,1,0:T(8,128)(2,1)} %bitcast.348), custom_call_target="tpu_custom_call" | custom-call | tf_op jit(solution)/shard_map/unpack_weights/pallas_call | solution.py:242
  203.0 9.0 %collective-permute-done.32 = f32[80,1024]{1,0:T(8,128)S(1)} collective-permute-done((f32[80,1024]{1,0:T(8,128)S(1)}, f32[80,1024]{1,0:T(8,128)S(1)}, u32[]{:S(2)}, u32[]{:S(2)}) %collective-permute-start.32) | collective-permute-done | bytes 327712 | tf_op jit(solution)/shard_map/ppermute | solution.py:42
  221.0 8.6 %collective-permute-done.35 = f32[80,1024]{1,0:T(8,128)} collective-permute-done((f32[80,1024]{1,0:T(8,128)}, f32[80,1024]{1,0:T(8,128)}, u32[]{:S(2)}, u32[]{:S(2)}) %collective-permute-start.35) | collective-permute-done | bytes 327712 | tf_op jit(solution)/shard_map/ppermute | solution.py:42
  245.4 9.0 %collective-permute-done.40 = f32[80,1024]{1,0:T(8,128)S(1)} collective-permute-done((f32[80,1024]{1,0:T(8,128)S(1)}, f32[80,1024]{1,0:T(8,128)S(1)}, u32[]{:S(2)}, u32[]{:S(2)}) %collective-permute-start.40) | collective-permute-done | bytes 327712 | tf_op jit(solution)/shard_map/ppermute | solution.py:42
  263.2 9.0 %collective-permute-done.43 = f32[80,1024]{1,0:T(8,128)S(1)} collective-permute-done((f32[80,1024]{1,0:T(8,128)S(1)}, f32[80,1024]{1,0:T(8,128)S(1)}, u32[]{:S(2)}, u32[]{:S(2)}) %collective-permute-start.43) | collective-permute-done | bytes 327712 | tf_op jit(solution)/shard_map/ppermute | solution.py:42
  323.1 14.3 %collective-permute-done.46 = f32[256,1024]{1,0:T(8,128)S(1)} collective-permute-done((f32[256,1024]{1,0:T(8,128)S(1)}, f32[256,1024]{1,0:T(8,128)S(1)}, u32[]{:S(2)}, u32[]{:S(2)}) %collective-permute-start.46) | collective-permute-done | bytes 1048608 | tf_op jit(solution)/shard_map/ppermute | solution.py:42
  346.2 10.1 %pack_gradients.1 = f32[192,128,128]{2,1,0:T(8,128)} custom-call(s32[192]{0:T(256)} %fusion.165.slots, f32[1024,768]{1,0:T(8,128)} %pad_maximum_fusion.1.refs_0_, f32[256,1024]{1,0:T(8,128)} %fusion.176.refs_1_, f32[1024,1024]{1,0:T(8,128)} %fusion.186.refs_2_, f32[1024,1024]{1,0:T(8,128)} %fusion.179.refs_3_), custom_call_target="tpu_custom_call" | custom-call | tf_op jit(solution)/shard_map/pack_gradients/pallas_call | solution.py:253
  356.3 12.7 %copy.139 = f32[8,24,128,128]{2,3,1,0:T(8,128)} copy(f32[8,24,128,128]{3,2,1,0:T(8,128)} %bitcast.347) | data formatting | bytes 25165824 | tf_op jit(solution)/shard_map/reshape | solution.py:447
  369.0 8.8 %convert.36 = bf16[8,24,128,128]{2,3,1,0:T(8,128)(2,1)} convert(f32[8,24,128,128]{2,3,1,0:T(8,128)} %copy.139) | non-fusion elementwise | flops 3145728 | bytes 18874368 | tf_op jit(solution)/shard_map/convert.15
  394.4 6.9 %fusion.1 = f32[1664,1024]{1,0:T(8,128)S(1)} fusion(s32[1024]{0:T(1024)S(1)} %copy-done.106, f32[1024]{0:T(1024)S(1)} %bitcast.406, f16[512,1024]{1,0:T(8,128)(2,1)} %collective-permute-done.67, f16[512,1024]{1,0:T(8,128)(2,1)} %maximum_select_fusion.2, pred[]{:T(512)S(6)} %eq.168), kind=kOutput, calls=%fused_computation.8 | convolution fusion | flops 3500802048 | bytes 8921089 | tf_op jit(solution)/shard_map/dot_general | solution.py:193
  401.5 6.9 %fusion.2 = f32[1664,1024]{1,0:T(8,128)S(1)} fusion(s32[1024]{0:T(1024)S(1)} %copy-done.106, f32[1024]{0:T(1024)S(1)} %bitcast.407, f16[512,1024]{1,0:T(8,128)(2,1)} %collective-permute-done.67, f16[512,1024]{1,0:T(8,128)(2,1)} %maximum_select_fusion.2, pred[]{:T(512)S(6)} %eq.168), kind=kOutput, calls=%fused_computation.9 | convolution fusion | flops 3497656320 | bytes 8921089 | tf_op jit(solution)/shard_map/dot_general | solution.py:193
  410.0 6.0 fusion.92
  448.6 5.8 fusion.194
  458.7 5.8 collective-permute-done.75
  486.7 6.3 collective-permute-done.78
  535.6 33.4 %all_gather.6 = f32[128,1024]{1,0:T(8,128)} all-gather(f32[16,1024]{1,0:T(8,128)S(1)} %get-tuple-element.279), channel_id=1, replica_groups=mesh['dp'=8,'mp'=4] {'dp'}, dimensions={0}, use_global_device_ids=true | all-gather | bytes 589824 | tf_op jit(solution)/shard_map/all_gather | solution.py:535
  596.5 6.1 fusion.17
  615.7 7.6 %multiply_subtract_fusion = (f32[526,1024]{1,0:T(8,128)}, f32[526,1024]{1,0:T(8,128)}, f32[526,1024]{1,0:T(8,128)}) fusion(f32[526,1024]{1,0:T(8,128)} %param.29, f32[]{:T(128)S(6)} %min.13, f32[14,1024]{1,0:T(8,128)S(1)} %get-tuple-element.284, f32[512,1024]{1,0:T(8,128)} %all-gather.2.cloned.1.call-done, f32[526,1024]{1,0:T(8,128)} %param.31, ...), kind=kLoop, calls=%fused_computation.30 | loop fusion | flops 7540736 | bytes 15081476 | tf_op jit(solution)/shard_map/sub | solution.py:176
  (639 shorter events, 387.6 us)
Async XLA Ops:
  7.2 608.5 %all-gather.2.cloned.1.call-start = ((), (), s32[]{:S(2)}) async-start(), calls=%async_computation | async-start | bytes 2621440 | tf_op jit(solution)/shard_map/all_gather | solution.py:534
  22.1 14.3 %collective-permute-start.4 = (bf16[112,1024]{1,0:T(8,128)(2,1)}, bf16[112,1024]{1,0:T(8,128)(2,1)S(1)}, u32[]{:S(2)}, u32[]{:S(2)}) collective-permute-start(bf16[112,1024]{1,0:T(8,128)(2,1)} %collective-permute-done.1), channel_id=1, source_target_pairs={{0,4},{4,0},{8,12},{12,8},{16,20},{20,16},{24,28},{28,24},{1,5},{5... | collective-permute-start | bytes 688136 | tf_op jit(solution)/shard_map/ppermute | solution.py:42
  50.3 14.2 %collective-permute-start.13 = (bf16[12,128,128]{2,1,0:T(8,128)(2,1)S(1)}, bf16[12,128,128]{2,1,0:T(8,128)(2,1)}, u32[]{:S(2)}, u32[]{:S(2)}) collective-permute-start(bf16[12,128,128]{2,1,0:T(8,128)(2,1)S(1)} %get-tuple-element.130), channel_id=1, source_target_pairs={{0,8},{4,12},{8,16},{12,20},{16,24},{20,28},{24,0},{28,4},{1,9},{5... | collective-permute-start | bytes 1179656 | tf_op jit(solution)/shard_map/ppermute | solution.py:47
  77.8 27.7 %collective-permute-start.17 = (bf16[512,1024]{1,0:T(8,128)(2,1)S(1)}, bf16[512,1024]{1,0:T(8,128)(2,1)S(1)}, u32[]{:S(2)}, u32[]{:S(2)}) collective-permute-start(bf16[512,1024]{1,0:T(8,128)(2,1)S(1)} %dynamic-slice_add_fusion.2), channel_id=1, source_target_pairs={{0,2},{1,3},{2,0},{3,1},{4,6},{5,7},{6,4},{7,5},{8,10},{9,11},{10,... | collective-permute-start | bytes 3145736 | tf_op jit(solution)/shard_map/ppermute | solution.py:42
  81.6 14.1 %collective-permute-start.22 = (bf16[12,128,128]{2,1,0:T(8,128)(2,1)}, bf16[12,128,128]{2,1,0:T(8,128)(2,1)}, u32[]{:S(2)}, u32[]{:S(2)}) collective-permute-start(bf16[12,128,128]{2,1,0:T(8,128)(2,1)} %collective-permute-done.15), channel_id=1, source_target_pairs={{0,8},{4,12},{8,16},{12,20},{16,24},{20,28},{24,0},{28,4},{1,9},{5... | collective-permute-start | bytes 1179656 | tf_op jit(solution)/shard_map/ppermute | solution.py:47
  81.6 14.1 %collective-permute-start.21 = (bf16[12,128,128]{2,1,0:T(8,128)(2,1)S(1)}, bf16[12,128,128]{2,1,0:T(8,128)(2,1)S(1)}, u32[]{:S(2)}, u32[]{:S(2)}) collective-permute-start(bf16[12,128,128]{2,1,0:T(8,128)(2,1)S(1)} %copy-done.59), channel_id=1, source_target_pairs={{0,4},{4,0},{8,12},{12,8},{16,20},{20,16},{24,28},{28,24},{1,5},{5... | collective-permute-start | bytes 1179656 | tf_op jit(solution)/shard_map/ppermute | solution.py:42
  82.2 21.9 %collective-permute-start.20 = (bf16[12,128,128]{2,1,0:T(8,128)(2,1)}, bf16[12,128,128]{2,1,0:T(8,128)(2,1)}, u32[]{:S(2)}, u32[]{:S(2)}) collective-permute-start(bf16[12,128,128]{2,1,0:T(8,128)(2,1)} %collective-permute-done.13), channel_id=1, source_target_pairs={{0,8},{4,12},{8,16},{12,20},{16,24},{20,28},{24,0},{28,4},{1,9},{5... | collective-permute-start | bytes 1179656 | tf_op jit(solution)/shard_map/ppermute | solution.py:47
  82.2 21.9 %collective-permute-start.19 = (bf16[12,128,128]{2,1,0:T(8,128)(2,1)S(1)}, bf16[12,128,128]{2,1,0:T(8,128)(2,1)S(1)}, u32[]{:S(2)}, u32[]{:S(2)}) collective-permute-start(bf16[12,128,128]{2,1,0:T(8,128)(2,1)S(1)} %get-tuple-element.130), channel_id=1, source_target_pairs={{0,4},{4,0},{8,12},{12,8},{16,20},{20,16},{24,28},{28,24},{1,5},{5... | collective-permute-start | bytes 1179656 | tf_op jit(solution)/shard_map/ppermute | solution.py:42
  95.7 22.7 %collective-permute-start.26 = (bf16[12,128,128]{2,1,0:T(8,128)(2,1)}, bf16[12,128,128]{2,1,0:T(8,128)(2,1)S(1)}, u32[]{:S(2)}, u32[]{:S(2)}) collective-permute-start(bf16[12,128,128]{2,1,0:T(8,128)(2,1)} %collective-permute-done.22), channel_id=1, source_target_pairs={{0,8},{4,12},{8,16},{12,20},{16,24},{20,28},{24,0},{28,4},{1,9},{5... | collective-permute-start | bytes 1179656 | tf_op jit(solution)/shard_map/ppermute | solution.py:47
  95.7 22.7 %collective-permute-start.25 = (bf16[12,128,128]{2,1,0:T(8,128)(2,1)}, bf16[12,128,128]{2,1,0:T(8,128)(2,1)}, u32[]{:S(2)}, u32[]{:S(2)}) collective-permute-start(bf16[12,128,128]{2,1,0:T(8,128)(2,1)} %collective-permute-done.15), channel_id=1, source_target_pairs={{0,4},{4,0},{8,12},{12,8},{16,20},{20,16},{24,28},{28,24},{1,5},{5... | collective-permute-start | bytes 1179656 | tf_op jit(solution)/shard_map/ppermute | solution.py:42
  104.1 15.7 %collective-permute-start.24 = (bf16[12,128,128]{2,1,0:T(8,128)(2,1)}, bf16[12,128,128]{2,1,0:T(8,128)(2,1)}, u32[]{:S(2)}, u32[]{:S(2)}) collective-permute-start(bf16[12,128,128]{2,1,0:T(8,128)(2,1)} %collective-permute-done.20), channel_id=1, source_target_pairs={{0,8},{4,12},{8,16},{12,20},{16,24},{20,28},{24,0},{28,4},{1,9},{5... | collective-permute-start | bytes 1179656 | tf_op jit(solution)/shard_map/ppermute | solution.py:47
  104.4 15.5 %collective-permute-start.23 = (bf16[12,128,128]{2,1,0:T(8,128)(2,1)}, bf16[12,128,128]{2,1,0:T(8,128)(2,1)}, u32[]{:S(2)}, u32[]{:S(2)}) collective-permute-start(bf16[12,128,128]{2,1,0:T(8,128)(2,1)} %collective-permute-done.13), channel_id=1, source_target_pairs={{0,4},{4,0},{8,12},{12,8},{16,20},{20,16},{24,28},{28,24},{1,5},{5... | collective-permute-start | bytes 1179656 | tf_op jit(solution)/shard_map/ppermute | solution.py:42
  105.9 57.6 %collective-permute-start.18 = (bf16[512,1024]{1,0:T(8,128)(2,1)S(1)}, bf16[512,1024]{1,0:T(8,128)(2,1)}, u32[]{:S(2)}, u32[]{:S(2)}) collective-permute-start(bf16[512,1024]{1,0:T(8,128)(2,1)S(1)} %add.785), channel_id=1, source_target_pairs={{0,1},{1,0},{2,3},{3,2},{4,5},{5,4},{6,7},{7,6},{8,9},{9,8},{10,11... | collective-permute-start | bytes 3145736 | tf_op jit(solution)/shard_map/ppermute | solution.py:42
  119.9 19.0 %collective-permute-start.27 = (bf16[12,128,128]{2,1,0:T(8,128)(2,1)}, bf16[12,128,128]{2,1,0:T(8,128)(2,1)S(1)}, u32[]{:S(2)}, u32[]{:S(2)}) collective-permute-start(bf16[12,128,128]{2,1,0:T(8,128)(2,1)} %collective-permute-done.20), channel_id=1, source_target_pairs={{0,4},{4,0},{8,12},{12,8},{16,20},{20,16},{24,28},{28,24},{1,5},{5... | collective-permute-start | bytes 1179656 | tf_op jit(solution)/shard_map/ppermute | solution.py:42
  130.5 16.9 %collective-permute-start.30 = (bf16[12,128,128]{2,1,0:T(8,128)(2,1)S(1)}, bf16[12,128,128]{2,1,0:T(8,128)(2,1)S(1)}, u32[]{:S(2)}, u32[]{:S(2)}) collective-permute-start(bf16[12,128,128]{2,1,0:T(8,128)(2,1)S(1)} %collective-permute-done.26), channel_id=1, source_target_pairs={{0,4},{4,0},{8,12},{12,8},{16,20},{20,16},{24,28},{28,24},{1,5},{5... | collective-permute-start | bytes 1179656 | tf_op jit(solution)/shard_map/ppermute | solution.py:42
  138.9 16.5 %collective-permute-start.29 = (bf16[12,128,128]{2,1,0:T(8,128)(2,1)}, bf16[12,128,128]{2,1,0:T(8,128)(2,1)S(1)}, u32[]{:S(2)}, u32[]{:S(2)}) collective-permute-start(bf16[12,128,128]{2,1,0:T(8,128)(2,1)} %collective-permute-done.24), channel_id=1, source_target_pairs={{0,4},{4,0},{8,12},{12,8},{16,20},{20,16},{24,28},{28,24},{1,5},{5... | collective-permute-start | bytes 1179656 | tf_op jit(solution)/shard_map/ppermute | solution.py:42
  312.2 25.3 %collective-permute-start.46 = (f32[256,1024]{1,0:T(8,128)S(1)}, f32[256,1024]{1,0:T(8,128)S(1)}, u32[]{:S(2)}, u32[]{:S(2)}) collective-permute-start(f32[256,1024]{1,0:T(8,128)S(1)} %constant_dynamic-slice_fusion), channel_id=1, source_target_pairs={{0,2},{1,3},{2,0},{3,1},{4,6},{5,7},{6,4},{7,5},{8,10},{9,11},{10,... | collective-permute-start | bytes 3145736 | tf_op jit(solution)/shard_map/ppermute | solution.py:42
  342.2 41.8 %collective-permute-start.66 = (f16[256,1024]{1,0:T(8,128)(2,1)S(1)}, f16[256,1024]{1,0:T(8,128)(2,1)}, u32[]{:S(2)}, u32[]{:S(2)}) collective-permute-start(f16[256,1024]{1,0:T(8,128)(2,1)S(1)} %divide_convert_fusion), channel_id=1, source_target_pairs={{0,2},{1,3},{2,0},{3,1},{4,6},{5,7},{6,4},{7,5},{8,10},{9,11},{10,... | collective-permute-start | bytes 1572872 | tf_op jit(solution)/shard_map/ppermute | solution.py:42
  392.7 29.5 %collective-permute-start.53 = (bf16[12,128,128]{1,2,0:T(8,128)(2,1)}, bf16[12,128,128]{1,2,0:T(8,128)(2,1)S(1)}, u32[]{:S(2)}, u32[]{:S(2)}) collective-permute-start(bf16[12,128,128]{1,2,0:T(8,128)(2,1)} %get-tuple-element.155), channel_id=1, source_target_pairs={{0,4},{4,0},{8,12},{12,8},{16,20},{20,16},{24,28},{28,24},{1,5},{5... | collective-permute-start | bytes 1179656 | tf_op jit(solution)/shard_map/ppermute | solution.py:42
  394.0 28.1 %collective-permute-start.54 = (bf16[12,128,128]{1,2,0:T(8,128)(2,1)S(1)}, bf16[12,128,128]{1,2,0:T(8,128)(2,1)S(1)}, u32[]{:S(2)}, u32[]{:S(2)}) collective-permute-start(bf16[12,128,128]{1,2,0:T(8,128)(2,1)S(1)} %fusion.61), channel_id=1, source_target_pairs={{0,8},{4,12},{8,16},{12,20},{16,24},{20,28},{24,0},{28,4},{1,9},{5... | collective-permute-start | bytes 1179656 | tf_op jit(solution)/shard_map/ppermute | solution.py:47
  457.5 15.4 %collective-permute-start.59 = (bf16[12,128,128]{1,2,0:T(8,128)(2,1)S(1)}, bf16[12,128,128]{1,2,0:T(8,128)(2,1)S(1)}, u32[]{:S(2)}, u32[]{:S(2)}) collective-permute-start(bf16[12,128,128]{1,2,0:T(8,128)(2,1)S(1)} %copy-done.55), channel_id=1, source_target_pairs={{0,4},{4,0},{8,12},{12,8},{16,20},{20,16},{24,28},{28,24},{1,5},{5... | collective-permute-start | bytes 1179656 | tf_op jit(solution)/shard_map/ppermute | solution.py:42
  476.7 16.4 %collective-permute-start.82 = (f16[112,1024]{1,0:T(8,128)(2,1)S(1)}, f16[112,1024]{1,0:T(8,128)(2,1)S(1)}, u32[]{:S(2)}, u32[]{:S(2)}) collective-permute-start(f16[112,1024]{1,0:T(8,128)(2,1)S(1)} %copy-done.65), channel_id=1, source_target_pairs={{0,4},{4,0},{8,12},{12,8},{16,20},{20,16},{24,28},{28,24},{1,5},{5... | collective-permute-start | bytes 688136 | tf_op jit(solution)/shard_map/ppermute | solution.py:42
  527.2 42.4 %collective-permute-start.64 = (bf16[12,128,128]{1,2,0:T(8,128)(2,1)S(1)}, bf16[12,128,128]{1,2,0:T(8,128)(2,1)}, u32[]{:S(2)}, u32[]{:S(2)}) collective-permute-start(bf16[12,128,128]{1,2,0:T(8,128)(2,1)S(1)} %copy-done.53), channel_id=1, source_target_pairs={{0,4},{4,0},{8,12},{12,8},{16,20},{20,16},{24,28},{28,24},{1,5},{5... | collective-permute-start | bytes 1179656 | tf_op jit(solution)/shard_map/ppermute | solution.py:42
  528.1 41.5 %collective-permute-start.65 = (bf16[12,128,128]{1,2,0:T(8,128)(2,1)}, bf16[12,128,128]{1,2,0:T(8,128)(2,1)}, u32[]{:S(2)}, u32[]{:S(2)}) collective-permute-start(bf16[12,128,128]{1,2,0:T(8,128)(2,1)} %fusion.57), channel_id=1, source_target_pairs={{0,8},{4,12},{8,16},{12,20},{16,24},{20,28},{24,0},{28,4},{1,9},{5... | collective-permute-start | bytes 1179656 | tf_op jit(solution)/shard_map/ppermute | solution.py:47
  (183 other events, 2001.4 us)
Sparse Core Ops, SparseCore 0:
  569.1 19.9 all-gather.1

commit v2 on v1

v2 whole, which is shorter than its diff:
```python
import functools
import math

import jax
import jax.numpy as jnp
from jax import lax
from jax.experimental import pallas as pl
from jax.experimental.pallas import tpu as pltpu
from jax.sharding import PartitionSpec as P

D = 1024
HEADS = 16
HD = 64
FF = 4096
VOC_DEV = 197
VOC_PAD = 208
LEN = 512
POS = 80
KB = 128
STRIP = 1664

HIGH = lax.Precision.HIGHEST
EPS_NORM = 1e-05
EPS_ADAM = 1e-08
BETA_FIRST = 0.5
BETA_SECOND = 0.5
RATE_ADAM = 0.01
RATE_SHAMPOO = 0.03
DECAY_TABLE = 0.01
DECAY_LAYER = 0.01
STAT_DECAY = 0.5
CLIP_FACTOR = 16.0
MASK_FILL = -1000000000.0
RING = 4
VMEM_SPARE = 60 << 20
VMEM_MOST = 60 << 20

f32 = jnp.float32
bf16 = jnp.bfloat16
f16 = jnp.float16


def swap(value, axis, ways, bit):
    pairs = [(i, i ^ bit) for i in range(ways)]
    return jax.tree.map(lambda part: lax.ppermute(part, axis, pairs), value)


def ring_step(value):
    pairs = [(i, (i + 2) % (2 * RING)) for i in range(2 * RING)]
    return lax.ppermute(value, "dp", pairs)


def after(values, *others):
    if not others:
        return values
    flat, tree = jax.tree.flatten(values)
    tied = lax.optimization_barrier(tuple(flat) + tuple(others))
    return jax.tree.unflatten(tree, tied[: len(flat)])


def along_x(value):
    return swap(value, "dp", 2 * RING, 1)


def fence(*values):
    return lax.optimization_barrier(values)


def half_float(value, bound=None):
    scale = power_scale(jnp.max(jnp.abs(value)) if bound is None else bound)
    return (value / scale).astype(f16), jnp.broadcast_to(scale, (1, 128))


def float_half(pair):
    return pair[0].astype(f32) * pair[1][0, 0]


def sum_halves(keep, send, ways):
    keep = keep + swap(send, "mp", ways, 1)
    keep = keep + swap(keep, "mp", ways, 2)
    return keep, swap(keep, "mp", ways, 1)


def near_sum(value, dp, mp):
    near = [swap(value, "mp", mp, bit) for bit in range(1, mp)]
    value = (value + near[0]) + (near[1] + near[2])
    return value + swap(value, "dp", dp, 1)


def far_sum(value, dp):
    far = [swap(value, "dp", dp, 2 * bit) for bit in range(1, RING)]
    return (value + far[0]) + (far[1] + far[2])


def butterfly(value, combine, dp, mp, both=True):
    axes = [("mp", mp)] + ([("dp", dp)] if both else [])
    for axis, ways in axes:
        bit = 1
        while bit < ways:
            value = combine(value, swap(value, axis, ways, bit))
            bit *= 2
    return value


def gelu_exact(values):
    return 0.5 * values * (1.0 + lax.erf(values * 0.7071067811865476))


def gelu_slope(values):
    cumulative = 0.5 * (1.0 + lax.erf(values * 0.7071067811865476))
    density = jnp.exp(-0.5 * values * values) * 0.3989422804014327
    return cumulative + values * density


def norm_forward(values, norm_gain, norm_shift):
    row_mean = jnp.mean(values, axis=-1, keepdims=True)
    centered = values - row_mean
    variance = jnp.mean(centered * centered, axis=-1, keepdims=True)
    inv_dev = lax.rsqrt(variance + EPS_NORM)
    normed = centered * inv_dev
    return (normed * norm_gain + norm_shift, normed, inv_dev)


def norm_backward(grad_out, normed, inv_dev, norm_gain):
    scaled = grad_out * norm_gain
    grad_in = inv_dev * (
        scaled
        - jnp.mean(scaled, axis=-1, keepdims=True)
        - normed * jnp.mean(scaled * normed, axis=-1, keepdims=True)
    )
    return (grad_in, jnp.sum(grad_out * normed, axis=0), jnp.sum(grad_out, axis=0))


def seq_ends_of(lengths):
    return jnp.stack(
        [jnp.sum(lengths[:, : s + 1], axis=1) for s in range(lengths.shape[1])], axis=1
    )


def positions_of(lengths):
    ends = seq_ends_of(lengths)
    places = jnp.arange(LEN, dtype=jnp.int32)
    passed = places[None, :, None] >= ends[:, None, :]
    segment = jnp.sum(passed.astype(jnp.int32), axis=2)
    start = jnp.max(jnp.where(passed, ends[:, None, :], 0), axis=2)
    return (segment, places[None, :] - start)


def adam_step(master, moment_one, moment_two, gradient, weight_decay):
    new_one = BETA_FIRST * moment_one + (1.0 - BETA_FIRST) * gradient
    new_two = BETA_SECOND * moment_two + (1.0 - BETA_SECOND) * gradient * gradient
    new_master = master - RATE_ADAM * (
        new_one / (jnp.sqrt(new_two) + EPS_ADAM) + weight_decay * master
    )
    return (new_master, new_one, new_two)


def product(left_side, right_side):
    return jnp.dot(left_side, right_side, preferred_element_type=f32)


def against_rows(left_side, right_side):
    return lax.dot_general(
        left_side, right_side, (((1,), (1,)), ((), ())), preferred_element_type=f32
    )


def over_rows(left_side, right_side):
    return lax.dot_general(
        left_side, right_side, (((0,), (0,)), ((), ())), preferred_element_type=f32
    )


def hit_matrix(codes, count, kind=bf16):
    return (codes[:, None] == jnp.arange(count, dtype=jnp.int32)[None, :]).astype(kind)


def split(values, parts):
    made = []
    for _ in range(parts):
        part = lax.reduce_precision(values, 8, 7)
        made.append(part.astype(bf16))
        values = values - part
    return made


def rows_exact(hits, values):
    upper, middle, lower = split(values, 3)
    return product(hits, upper) + product(hits, middle) + product(hits, lower)


def power_scale(bound):
    safe = jnp.clip(bound, 1e-30, 1e38)
    return jnp.exp2(jnp.ceil(jnp.log2(safe)) - 14.0)


SMEM = pl.BlockSpec(memory_space=pltpu.SMEM)
VMEM = pl.BlockSpec(memory_space=pltpu.VMEM)
ANY = pl.BlockSpec(memory_space=pl.ANY)


def params(*arrays, spare=VMEM_SPARE):
    total = spare
    for one in arrays:
        *lead, rows, columns = one.shape
        size = jnp.dtype(one.dtype).itemsize
        tile = 32 // size
        total += math.prod(lead) * -(-rows // tile) * tile * -(-columns // 128) * 128 * size
    return pltpu.CompilerParams(vmem_limit_bytes=min(total, VMEM_MOST))


COST = pl.CostEstimate(flops=1, bytes_accessed=1, transcendentals=0)


def shape(dims, kind=f32):
    return jax.ShapeDtypeStruct(dims, kind)


def call(kernel, outs, scalars, arrays, name, scratch=(), spare=VMEM_SPARE):
    return pl.pallas_call(
        kernel,
        out_shape=outs,
        in_specs=[SMEM] * len(scalars) + [VMEM] * len(arrays),
        out_specs=jax.tree.map(lambda _: VMEM, outs),
        scratch_shapes=list(scratch),
        compiler_params=params(*jax.tree.leaves(outs), *arrays, *scratch, spare=spare),
        cost_estimate=COST,
        name=name,
    )(*scalars, *arrays)


def both_halves(mine, other):
    return jnp.concatenate([mine, other], axis=0)


def part_halves(value, keep, send):
    half = value.shape[0] // 2
    keep[...] = value[:half]
    send[...] = value[half:]


def strips(pieces):
    base = 0
    for piece in pieces:
        for start in range(0, piece.shape[0], STRIP):
            size = min(STRIP, piece.shape[0] - start)
            yield base + start, piece, slice(start, start + size)
        base += piece.shape[0]


def embed_kernel(codes, *refs):
    pieces, words, table = refs[:-2], refs[-2], refs[-1]
    for base, piece, rows in strips(pieces):
        table[base : base + rows.stop - rows.start, :] = piece[rows, :]
    step = 256
    for begin in range(0, words.shape[0], step):
        part = slice(begin, begin + step)
        column = lax.broadcasted_iota(jnp.int32, (step, table.shape[0]), 1)
        hits = jnp.where(codes[part, :] == column, 1.0, 0.0).astype(bf16)
        words[part, :] = product(hits, table[...]).astype(bf16)


def embed_strips_kernel(codes, piece, words, total):
    step = pl.program_id(0)

    @pl.when(step == 0)
    def _():
        total[...] = jnp.zeros_like(total)

    size = piece.shape[0]
    column = lax.broadcasted_iota(jnp.int32, (codes.shape[0], size), 1) + step * size
    hits = jnp.where(codes[...] == column, 1.0, 0.0).astype(bf16)
    total[...] += product(hits, piece[...])

    @pl.when(step == pl.num_programs(0) - 1)
    def _():
        words[...] = total[...].astype(bf16)


def embed(codes, pieces):
    tokens = codes.shape[0]
    out = shape((tokens, D), bf16)
    if len(pieces) > 1:
        vocab = sum(piece.shape[0] for piece in pieces)
        scratch = [pltpu.VMEM((vocab, D), bf16)]
        return call(embed_kernel, out, [], [codes, *pieces], "embed", scratch, VMEM_MOST)
    return pl.pallas_call(
        embed_strips_kernel,
        grid=(pieces[0].shape[0] // STRIP,),
        out_shape=out,
        in_specs=[
            pl.BlockSpec((tokens, 1), lambda r: (0, 0)),
            pl.BlockSpec((STRIP, D), lambda r: (r, 0)),
        ],
        out_specs=pl.BlockSpec((tokens, D), lambda r: (0, 0)),
        scratch_shapes=[pltpu.VMEM((tokens, D), f32)],
        compiler_params=pltpu.CompilerParams(vmem_limit_bytes=32 << 20),
        cost_estimate=COST,
        name="embed",
    )(codes, *pieces)


def normalize_kernel(flat, words, places, affine, x_low, picked, picked_low, *rest):
    x_out = rest[-1]
    step = 128
    for begin in range(0, words.shape[0], step):
        part = slice(begin, begin + step)
        out, _, _ = norm_forward(
            words[part, :].astype(f32) + places[part, :], affine[0:1, :], affine[1:2, :]
        )
        x_out[part, :] = out
        x_low[part, :] = out.astype(bf16)

    def pick_row(p, carry):
        picked[pl.ds(p, 1), :] = x_out[pl.ds(flat[p], 1), :]
        return carry

    lax.fori_loop(0, picked.shape[0], pick_row, 0, unroll=8)
    picked_low[...] = picked[...].astype(bf16)


def head_pair(values, lanes):
    zero = jnp.zeros_like(values)
    return jnp.concatenate([jnp.where(lanes, values, zero), jnp.where(lanes, zero, values)], axis=0)


def attend_kernel(groups, downs, acrosses, *refs):
    pieces, refs = refs[:groups], refs[groups:]
    (
        x_mine,
        x_other,
        picked_mine,
        picked_other,
        bias_query,
        bias_keyval,
        segment,
        pick_segment,
        joined_w,
        output_w,
        upward_w,
        downward_w,
        keyval,
        query,
        probs,
        mixed,
        keep,
        send,
        stacked,
        dense,
        x_low,
        sems,
        out_sems,
    ) = refs
    rows = segment.shape[0]
    inner = query.shape[1]
    hidden = upward_w.shape[1]
    each = pieces[0].shape[0]
    loads = [
        pltpu.make_async_copy(piece, stacked.at[pl.ds(g * each, each)], sems.at[g])
        for g, piece in enumerate(pieces)
    ]
    half = x_low.shape[0] // 2
    loads_x = [
        pltpu.make_async_copy(x_mine, x_low.at[pl.ds(0, half)], sems.at[groups]),
        pltpu.make_async_copy(x_other, x_low.at[pl.ds(half, half)], sems.at[groups + 1]),
    ]
    for load in loads + loads_x:
        load.start()
    for g, load in enumerate(loads):
        load.wait()
        for t in range(g * each, (g + 1) * each):
            down = pl.multiple_of(downs[t], KB)
            across = pl.multiple_of(acrosses[t], KB)
            dense[pl.ds(down, KB), pl.ds(across, KB)] = stacked[t]
    start_up, start_down = 3 * inner, 3 * inner + hidden
    stores = [
        pltpu.make_async_copy(dense.at[down, across], out, out_sems.at[n])
        for n, (out, down, across) in enumerate(
            (
                (joined_w, pl.ds(0, D), pl.ds(0, start_up)),
                (output_w, pl.ds(D, inner), pl.ds(0, D)),
                (upward_w, pl.ds(0, D), pl.ds(start_up, hidden)),
                (downward_w, pl.ds(0, hidden), pl.ds(start_down, D)),
            )
        )
    ]
    for store in stores:
        store.start()
    for load in loads_x:
        load.wait()
    pairs = inner // KB
    picked_low = both_halves(picked_mine[...], picked_other[...])
    query[...] = (product(picked_low, dense[:D, :inner]) + bias_query[...]).astype(bf16)
    lanes = lax.broadcasted_iota(jnp.int32, (POS, KB), 1) < HD
    for r in range(rows):
        part = slice(r * LEN, (r + 1) * LEN)
        picks = slice(r * POS, (r + 1) * POS)
        keyval[part, :] = (
            product(x_low[part, :], dense[:D, inner:start_up]) + bias_keyval[...]
        ).astype(bf16)
        same = pick_segment[picks, :] == segment[r : r + 1, :]
        same = jnp.concatenate([same, same], axis=0)
        for pair in range(pairs):
            cut = slice(pair * KB, (pair + 1) * KB)
            cut_v = slice(inner + pair * KB, inner + (pair + 1) * KB)
            both = head_pair(query[picks, cut], lanes)
            scores = against_rows(both, keyval[part, cut]) * HD ** (-0.5)
            scores = jnp.where(same, scores, MASK_FILL)
            raised = jnp.exp(scores - jnp.max(scores, axis=-1, keepdims=True))
            part_probs = raised / jnp.sum(raised, axis=-1, keepdims=True)
            probs[r * pairs + pair] = part_probs
            out = product(part_probs.astype(bf16), keyval[part, cut_v])
            mixed[picks, cut] = jnp.where(lanes, out[:POS], out[POS:]).astype(bf16)
    part_halves(product(mixed[...], dense[D:, :D]), keep, send)
    for store in stores:
        store.wait()


def attend(corners, pieces, x_halves, picked_halves, bias_query, bias_keyval, segment, pick_segment, hidden):
    rows = segment.shape[0]
    inner = bias_query.shape[1]
    tokens, picks = 2 * x_halves[0].shape[0], 2 * picked_halves[0].shape[0]
    groups = len(pieces)
    total = groups * pieces[0].shape[0]
    scratch = [
        pltpu.VMEM((total, KB, KB), bf16),
        pltpu.VMEM((D + inner, 3 * inner + 2 * hidden), bf16),
        pltpu.VMEM((tokens, D), bf16),
    ]
    outs = [
            shape((D, 3 * inner), bf16),
            shape((inner, D), bf16),
            shape((D, hidden), bf16),
            shape((hidden, D), bf16),
            shape((tokens, 2 * inner), bf16),
            shape((picks, inner), bf16),
            shape((rows * inner // KB, 2 * POS, LEN)),
            shape((picks, inner), bf16),
            shape((picks // 2, D)),
            shape((picks // 2, D)),
    ]
    return pl.pallas_call(
        functools.partial(attend_kernel, groups),
        out_shape=outs,
        in_specs=[SMEM] * 2 + [ANY] * (groups + 2) + [VMEM] * 6,
        out_specs=[ANY] * 4 + [VMEM] * 6,
        scratch_shapes=scratch
        + [pltpu.SemaphoreType.DMA((groups + 2,)), pltpu.SemaphoreType.DMA((4,))],
        compiler_params=params(spare=VMEM_MOST),
        cost_estimate=COST,
        name="attend",
    )(*corners, *pieces, *x_halves, *picked_halves, bias_query, bias_keyval, segment, pick_segment)


def forward_kernel(
    mine,
    other,
    picked_mine,
    picked_other,
    affine,
    bias_up,
    upward_w,
    downward_w,
    normed_out,
    inv_out,
    first,
    first_low,
    upper_pre,
    acted,
    keep,
    send,
):
    attended = both_halves(mine[...], other[...]) + affine[0:1, :]
    out, normed, inv = norm_forward(
        both_halves(picked_mine[...], picked_other[...]) + attended,
        affine[1:2, :],
        affine[2:3, :],
    )
    normed_out[...] = normed
    inv_out[...] = inv
    first[...] = out
    first_low[...] = out.astype(bf16)
    upper = product(first_low[...], upward_w[...]) + bias_up[...]
    upper_pre[...] = upper
    acted[...] = gelu_exact(upper).astype(bf16)
    part_halves(product(acted[...], downward_w[...]), keep, send)


def logits_kernel(mine, other, first, affine, target, *refs):
    pieces, refs = refs[:-6], refs[-6:]
    normed_out, inv_out, picked_low, top_feature, logits, stats = refs
    branch = both_halves(mine[...], other[...]) + affine[0:1, :]
    out, normed, inv = norm_forward(first[...] + branch, affine[1:2, :], affine[2:3, :])
    normed_out[...] = normed
    inv_out[...] = inv
    picked_low[...] = out.astype(bf16)
    top_feature[...] = jnp.broadcast_to(jnp.max(jnp.abs(out)), top_feature.shape)
    count = out.shape[0]
    top = jnp.full((1, count), -jnp.inf, f32)
    chosen = jnp.zeros((1, count), f32)
    for base, piece, rows in strips(pieces):
        size = rows.stop - rows.start
        part = against_rows(piece[rows, :], picked_low[...])
        row = lax.broadcasted_iota(jnp.int32, (size, count), 0) + base
        part = jnp.where(row % VOC_PAD < VOC_DEV, part, -jnp.inf)
        logits[base : base + size, :] = part
        top = jnp.maximum(top, jnp.max(part, axis=0, keepdims=True))
        hit = jnp.where(row == target[...], part, 0.0)
        chosen = chosen + jnp.sum(hit, axis=0, keepdims=True)
    total = jnp.zeros((1, count), f32)
    for base, piece, rows in strips(pieces):
        part = logits[base : base + rows.stop - rows.start, :]
        total = total + jnp.sum(jnp.exp(part - top), axis=0, keepdims=True)
    stats[0:1, :] = top
    stats[1:2, :] = total
    stats[2:3, :] = chosen
    stats[3:8, :] = jnp.zeros((5, count), f32)


def head_kernel(own, near, far, across, target, logits, *refs):
    pieces, refs = refs[:-4], refs[-4:]
    grad_logits, loss, keep, send = refs
    count = target.shape[1]
    middle = count // 2

    def turned(one):
        return jnp.concatenate([one[:, middle:], one[:, :middle]], axis=1)

    everyone = (own[...], turned(near[...]), far[...], turned(across[...]))
    top = functools.reduce(jnp.maximum, [one[0:1, :] for one in everyone])
    parts = [one[1:2, :] * jnp.exp(one[0:1, :] - top) for one in everyone]
    total = (parts[0] + parts[1]) + (parts[2] + parts[3])
    chosen = [one[2:3, :] for one in everyone]
    chosen = (chosen[0] + chosen[1]) + (chosen[2] + chosen[3])
    losses = jnp.sum(jnp.log(total) + top - chosen, axis=1, keepdims=True)
    loss[...] = jnp.broadcast_to(losses, loss.shape)
    back = jnp.zeros((count, D), f32)
    for base, piece, rows in strips(pieces):
        size = rows.stop - rows.start
        row = lax.broadcasted_iota(jnp.int32, (size, count), 0) + base
        hit = jnp.where(row == target[...], 1.0, 0.0)
        part = logits[base : base + size, :]
        part = (jnp.exp(part - top) / total - hit).astype(bf16)
        grad_logits[base : base + size, :] = part
        back = back + over_rows(part, piece[rows, :])
    part_halves(back, keep, send)


def backward_kernel(
    mine,
    other,
    normed,
    inv,
    gain,
    upper_pre,
    upward_w,
    downward_w,
    grad_pre2,
    branch_grad,
    upper_grad,
    row_sums,
    upper_sums,
    keep,
    send,
):
    grad_out = both_halves(mine[...], other[...])
    grad_in, gain_sum, shift_sum = norm_backward(grad_out, normed[...], inv[...], gain[...])
    grad_pre2[...] = grad_in
    branch_grad[...] = grad_in.astype(bf16)
    row_sums[0:1, :] = gain_sum[None]
    row_sums[1:2, :] = shift_sum[None]
    row_sums[2:3, :] = jnp.sum(branch_grad[...].astype(f32), axis=0, keepdims=True)
    upper = against_rows(branch_grad[...], downward_w[...]) * gelu_slope(upper_pre[...])
    upper_grad[...] = upper.astype(bf16)
    upper_sums[...] = jnp.sum(upper_grad[...].astype(f32), axis=0, keepdims=True)
    part_halves(against_rows(upper_grad[...], upward_w[...]), keep, send)


def back_attention_kernel(
    positions,
    rank_first,
    mine,
    other,
    grad_pre2,
    first_normed,
    first_inv,
    gain,
    joined_w,
    output_w,
    keyval,
    query,
    probs,
    keep,
    send,
    row_sums,
    query_sums,
    keyval_sums,
    attended_grad,
    query_grad,
    keyval_grad,
    pick_grad,
):
    picks, inner = query.shape
    rows = picks // POS
    pairs = inner // KB
    scale = HD ** (-0.5)
    grad_out = both_halves(mine[...], other[...]) + grad_pre2[...]
    grad_pre1, gain_sum, shift_sum = norm_backward(
        grad_out, first_normed[...], first_inv[...], gain[...]
    )
    attended_grad[...] = grad_pre1.astype(bf16)
    row_sums[0:1, :] = gain_sum[None]
    row_sums[1:2, :] = shift_sum[None]
    row_sums[2:3, :] = jnp.sum(attended_grad[...].astype(f32), axis=0, keepdims=True)
    mixed_grad = against_rows(attended_grad[...], output_w[...]).astype(bf16)
    lanes = lax.broadcasted_iota(jnp.int32, (POS, KB), 1) < HD
    for r in range(rows):
        part = slice(r * LEN, (r + 1) * LEN)
        here = slice(r * POS, (r + 1) * POS)
        for pair in range(pairs):
            cut = slice(pair * KB, (pair + 1) * KB)
            cut_v = slice(inner + pair * KB, inner + (pair + 1) * KB)
            part_probs = probs[r * pairs + pair]
            out_grad = head_pair(mixed_grad[here, cut], lanes)
            both = head_pair(query[here, cut], lanes)
            probs_grad = against_rows(out_grad, keyval[part, cut_v])
            inner_sum = jnp.sum(probs_grad * part_probs, axis=-1, keepdims=True)
            scores_grad = (part_probs * (probs_grad - inner_sum)).astype(bf16)
            back = product(scores_grad, keyval[part, cut])
            query_grad[here, cut] = (jnp.where(lanes, back[:POS], back[POS:]) * scale).astype(bf16)
            keyval_grad[part, cut] = (over_rows(scores_grad, both) * scale).astype(bf16)
            keyval_grad[part, cut_v] = over_rows(part_probs.astype(bf16), out_grad).astype(bf16)
    query_sums[...] = jnp.sum(query_grad[...].astype(f32), axis=0, keepdims=True)
    keyval_sums[...] = jnp.sum(keyval_grad[...].astype(f32), axis=0, keepdims=True)
    pick_grad[...] = (
        against_rows(query_grad[...], joined_w[:, :inner]) + grad_pre1 * rank_first[0]
    )
    for row, out in ((1, send), (0, keep)):
        out[...] = against_rows(keyval_grad[row * LEN : (row + 1) * LEN, :], joined_w[:, inner:])

        def add_row(p, carry):
            spot = positions[row * POS + p]
            out[pl.ds(spot, 1), :] += pick_grad[pl.ds(row * POS + p, 1), :]
            return carry

        lax.fori_loop(0, POS, add_row, 0, unroll=8)


def back_weights_kernel(
    downs,
    acrosses,
    x_mine,
    x_other,
    keyval_grad,
    picked_mine,
    picked_other,
    query_grad,
    mixed,
    attended_grad,
    acted,
    branch_grad,
    first_low,
    upper_grad,
    *rest,
):
    packed, dense = rest[:-1], rest[-1]
    inner = query_grad.shape[1]
    low = dense.dtype
    picked_low = both_halves(picked_mine[...], picked_other[...])
    dense[:D, :inner] = over_rows(picked_low, query_grad[...]).astype(low)
    half = x_mine.shape[0]
    joined = over_rows(x_mine[...], keyval_grad[:half, :])
    joined = joined + over_rows(x_other[...], keyval_grad[half:, :])
    dense[:D, inner : 3 * inner] = joined.astype(low)
    start_up, start_down = 3 * inner, 3 * inner + upper_grad.shape[1]
    dense[:D, start_up:start_down] = over_rows(first_low[...], upper_grad[...]).astype(low)
    dense[:D, start_down:] = over_rows(acted[...], branch_grad[...]).astype(low)
    dense[D:, :D] = over_rows(mixed[...], attended_grad[...]).astype(low)
    spot = 0
    for out in packed:
        for t in range(out.shape[0]):
            down = pl.multiple_of(downs[spot], KB)
            across = pl.multiple_of(acrosses[spot], KB)
            out[t] = dense[pl.ds(down, KB), pl.ds(across, KB)]
            spot += 1


def tile_corners(natural, inner, hidden):
    count_joined, count_output = D // KB * 3 * inner // KB, inner // KB * D // KB
    count_up = D // KB * hidden // KB
    n_joined = natural
    n_output = natural - count_joined
    n_up = n_output - count_output
    n_down = n_up - count_up
    wide_joined, wide, wide_up = 3 * inner // KB, D // KB, hidden // KB
    down = jnp.where(
        n_output < 0,
        n_joined // wide_joined * KB,
        jnp.where(
            n_up < 0,
            D + n_output // wide * KB,
            jnp.where(n_down < 0, n_up // wide_up * KB, n_down // wide * KB),
        ),
    )
    across = jnp.where(
        n_output < 0,
        n_joined % wide_joined * KB,
        jnp.where(
            n_up < 0,
            n_output % wide * KB,
            jnp.where(
                n_down < 0,
                3 * inner + n_up % wide_up * KB,
                3 * inner + hidden + n_down % wide * KB,
            ),
        ),
    )
    return down, across


def embedding_kernel(keep, came, words, places, gain, grad, sums, top):
    _, normed, inv = norm_forward(words[...].astype(f32) + places[...], gain[...], gain[...])
    grad_in, gain_sum, shift_sum = norm_backward(
        keep[...] + came[...], normed, inv, gain[...]
    )
    grad[...] = grad_in
    sums[0:1, :] = gain_sum[None]
    sums[1:2, :] = shift_sum[None]
    top[...] = jnp.broadcast_to(jnp.max(jnp.abs(grad_in)), top.shape)


def place_kernel(codes, upper, lower, grad):
    rows = grad.shape[0]
    hits = lax.broadcasted_iota(jnp.int32, (rows, codes.shape[1]), 0) == codes[...]
    hits = jnp.where(hits, 1.0, 0.0).astype(bf16)
    grad[...] = product(hits, upper[...]) + product(hits, lower[...])


def table_kernel(codes, upper, lower, grad_logits, picked_low, grad, hits):
    @pl.when(pl.program_id(1) == 0)
    def _():
        rows = grad.shape[0]
        row = lax.broadcasted_iota(jnp.int32, hits.shape, 0) + pl.program_id(0) * rows
        hits[...] = jnp.where(row == codes[...], 1.0, 0.0).astype(bf16)

    total = product(hits[...], upper[...]) + product(hits[...], lower[...])
    grad[...] = total + product(grad_logits[...], picked_low[...])


def table_gradient(codes, upper, lower, grad_logits, picked_low):
    vocab, picks = grad_logits.shape
    tokens = upper.shape[0]
    wide = 256

    def columns(high):
        return pl.BlockSpec((high, wide), lambda r, c: (0, c))

    return pl.pallas_call(
        table_kernel,
        grid=(vocab // STRIP, D // wide),
        out_shape=shape((vocab, D)),
        in_specs=[
            pl.BlockSpec((1, tokens), lambda r, c: (0, 0)),
            columns(tokens),
            columns(tokens),
            pl.BlockSpec((STRIP, picks), lambda r, c: (r, 0)),
            columns(picks),
        ],
        out_specs=pl.BlockSpec((STRIP, wide), lambda r, c: (r, c)),
        scratch_shapes=[pltpu.VMEM((STRIP, tokens), bf16)],
        compiler_params=params(),
        cost_estimate=COST,
        name="table_gradient",
    )(codes, upper, lower, grad_logits, picked_low)


def local(
    input_ids,
    seq_lengths,
    loss_positions,
    targets,
    block_owner,
    layer_master,
    stats_left,
    stats_right,
    root_left,
    root_right,
    table_master,
    table_first,
    table_second,
    vector_master,
    vector_first,
    vector_second,
):
    mp = lax.axis_size("mp")
    dp = lax.axis_size("dp")
    fast = dp == 2 * RING
    model_rank = lax.axis_index("mp")
    data_rank = lax.axis_index("dp")
    inner = D // mp
    ff_rows = FF // D
    hidden = FF // mp
    rows = input_ids.shape[0]
    tokens = rows * LEN
    share = tokens // mp
    own_blocks = layer_master.shape[1]
    blocks = own_blocks * dp

    if fast:
        z_here, x_here = data_rank // 2, data_rank % 2

        def place_of(owner):
            return 2 * ((z_here - owner // 2) % RING) + (owner % 2 + x_here) % 2
    else:

        def place_of(owner):
            return owner

    low_bit, high_bit = model_rank % 2, model_rank // 2

    def turned(array):
        return jnp.where(low_bit == 0, array, array[::-1])

    input_ids, seq_lengths = turned(input_ids), turned(seq_lengths)
    loss_positions, targets = turned(loss_positions), turned(targets)
    rank_first = (model_rank == 0).astype(f32)
    tail = vector_master[LEN:]
    bias_query = lax.dynamic_slice_in_dim(tail[2], model_rank * inner, inner)[None]
    bias_value = lax.dynamic_slice_in_dim(tail[3], model_rank * inner, inner)
    bias_keyval = jnp.concatenate([jnp.zeros((inner,), f32), bias_value])[None]
    bias_up = lax.dynamic_slice_in_dim(tail[7 : 7 + ff_rows].reshape(FF), model_rank * hidden, hidden)[None]
    affine_one = tail[4:7]
    affine_two = tail[7 + ff_rows : 10 + ff_rows]

    segment, offset = positions_of(seq_lengths)
    pick_segment = jnp.sum(
        (seq_ends_of(seq_lengths)[:, None, :] <= loss_positions[:, :, None]).astype(jnp.int32), axis=2
    ).reshape(-1, 1)

    def codes_of(ids):
        part = ids // VOC_DEV
        code = place_of(part // mp) * VOC_PAD + ids % VOC_DEV
        return jnp.where(part % mp == model_rank, code, -1)

    codes = codes_of(input_ids.reshape(-1))
    target_codes = codes_of(targets.reshape(1, -1))

    def corners_of():
        number = jnp.arange(blocks, dtype=jnp.int32)
        if fast:
            part = number // own_blocks
            owner = 2 * ((z_here - part // 2) % RING) + (part % 2 + x_here) % 2
            taken = owner * own_blocks + number % own_blocks
            order = jnp.sum(
                jnp.where(taken[:, None] == number[None, :], block_owner[None, :], 0), axis=1
            )
        else:
            order = block_owner
        return tile_corners(order, inner, hidden)

    table_low = jnp.pad(table_master.astype(bf16), ((0, VOC_PAD - VOC_DEV), (0, 0)))
    layer_low = layer_master[0].astype(bf16)
    vocab = dp * VOC_PAD
    words_half = tokens // 2
    def places_of(row):
        return rows_exact(hit_matrix(offset[row], LEN), vector_master[:LEN])

    def normalize(row, words):
        return call(
            normalize_kernel,
            [
                shape((words_half, D), bf16),
                shape((POS, D)),
                shape((POS, D), bf16),
            ],
            [loss_positions[row]],
            [words, places[row], tail[0:2]],
            "normalize",
            [pltpu.VMEM((words_half, D), f32)],
        )

    send_codes, keep_codes = codes[words_half:, None], codes[:words_half, None]
    if fast:
        held, crossed = [table_low], []
        places = []
        for k in range(RING - 1):
            made = [places_of(k)] if k < rows else []
            moved, met, made = fence(ring_step(held[k]), along_x(held[k]), made)
            held.append(moved)
            crossed.append(met)
            places += made
            held[-1], layer_low = fence(held[-1], layer_low)
        moved, met, last = fence(
            ring_step(layer_low), along_x(layer_low), along_x(held[RING - 1])
        )
        crossed.append(last)
        table_parts = [piece for pair in zip(held, crossed) for piece in pair]
        held, crossed = [layer_low, moved], [met]
        send = embed(send_codes, table_parts)
        near = swap(send, "mp", mp, 1)
        keep = embed(keep_codes, table_parts) + near
        moved, met, keep = fence(ring_step(held[1]), along_x(held[1]), keep)
        held.append(moved)
        crossed.append(met)
        far = swap(keep, "mp", mp, 2)
        moved, met, keep, far = fence(ring_step(held[2]), along_x(held[2]), keep, far)
        held.append(moved)
        crossed.append(met)
        words = keep + far
        near = swap(words, "mp", mp, 1)
        x_mine, x_other = normalize(0, words), normalize(1, near)
        met, x_mine, x_other = fence(along_x(held[3]), x_mine, x_other)
        crossed.append(met)
        layer_parts = [piece for pair in zip(held, crossed) for piece in pair]
    else:
        places = [places_of(row) for row in range(rows)]
        table_parts = [lax.all_gather(table_low, "dp", axis=0, tiled=True)]
        layer_parts = [lax.all_gather(layer_low, "dp", axis=0, tiled=True)]
        keep, send = embed(keep_codes, table_parts), embed(send_codes, table_parts)
        words, near = sum_halves(keep, send, mp)
        x_mine, x_other = normalize(0, words), normalize(1, near)

    (
        joined_w,
        output_w,
        upward_w,
        downward_w,
        keyval,
        queries,
        probs,
        mixed_low,
        keep,
        send,
    ) = attend(
        corners_of(),
        layer_parts,
        [x_mine[0], x_other[0]],
        [x_mine[2], x_other[2]],
        bias_query,
        bias_keyval,
        segment,
        pick_segment,
        hidden,
    )
    count = rows * POS
    half_shapes = [shape((count // 2, D)), shape((count // 2, D))]
    row_shape, low_shape = shape((count, D)), shape((count, D), bf16)
    first_normed, first_inv, first_out, first_low, upper_pre, acted_low, keep, send = call(
        forward_kernel,
        [
            row_shape,
            shape((count, 1)),
            row_shape,
            low_shape,
            shape((count, hidden)),
            shape((count, hidden), bf16),
            *half_shapes,
        ],
        [],
        [*sum_halves(keep, send, mp), x_mine[1], x_other[1], affine_one, bias_up, upward_w, downward_w],
        "forward",
    )

    second_normed, second_inv, picked_low, top_feature, logits, stats = call(
        logits_kernel,
        [
            row_shape,
            shape((count, 1)),
            low_shape,
            shape((1, 128)),
            shape((vocab, count)),
            shape((8, count)),
        ],
        [],
        [*sum_halves(keep, send, mp), first_out, affine_two, target_codes, *table_parts],
        "logits",
    )
    everyone = [stats] + [swap(stats, "mp", mp, bit) for bit in range(1, mp)]
    grad_logits, loss_part, keep, send = call(
        head_kernel,
        [shape((vocab, count), bf16), shape((1, 128)), *half_shapes],
        [],
        [*everyone, target_codes, logits, *table_parts],
        "head",
    )

    grad_pre2, branch_grad, upper_grad, sums_two, upper_sums, keep, send = call(
        backward_kernel,
        [
            row_shape,
            low_shape,
            shape((count, hidden), bf16),
            shape((3, D)),
            shape((1, hidden)),
            *half_shapes,
        ],
        [],
        [
            *sum_halves(keep, send, mp),
            second_normed,
            second_inv,
            affine_two[1:2],
            upper_pre,
            upward_w,
            downward_w,
        ],
        "backward",
    )
    keep, send, sums_one, query_sums, keyval_sums, attended_grad, query_grad, keyval_grad = call(
        back_attention_kernel,
        [
            shape((tokens // 2, D)),
            shape((tokens // 2, D)),
            shape((3, D)),
            shape((1, inner)),
            shape((1, 2 * inner)),
            low_shape,
            shape((count, inner), bf16),
            shape((tokens, 2 * inner), bf16),
        ],
        [loss_positions.reshape(-1), rank_first.reshape(1)],
        [
            *sum_halves(keep, send, mp),
            grad_pre2,
            first_normed,
            first_inv,
            affine_one[1:2],
            joined_w,
            output_w,
            keyval,
            queries,
            probs,
        ],
        "back_attention",
        [pltpu.VMEM((count, D), f32)],
        VMEM_MOST,
    )
    groups = dp if fast else 1
    layer_grad = call(
        back_weights_kernel,
        [shape((blocks // groups, KB, KB), bf16)] * groups,
        corners_of(),
        [
            x_mine[0],
            x_other[0],
            keyval_grad,
            x_mine[2],
            x_other[2],
            query_grad,
            mixed_low,
            attended_grad,
            acted_low,
            branch_grad,
            first_low,
            upper_grad,
        ],
        "back_weights",
        [pltpu.VMEM((D + inner, 3 * inner + 2 * hidden), bf16)],
        VMEM_MOST,
    )

    def quarters_of(value):
        return (
            lax.dynamic_slice_in_dim(value, high_bit * share, share, 0),
            lax.dynamic_slice_in_dim(value, (1 - high_bit) * share, share, 0),
        )

    own_words = lax.dynamic_slice_in_dim(words, high_bit * share, share, 0)
    own_places = lax.dynamic_slice_in_dim(places[0], high_bit * share, share, 0)

    def embedding(keep, came):
        return call(
            embedding_kernel,
            [shape((share, D)), shape((2, D)), shape((1, 128))],
            [],
            [keep, came, own_words, own_places, tail[0:1]],
            "embedding",
        )

    def ordered(one, two, bit):
        return jax.tree.map(
            lambda a, b: jnp.where(
                bit == 0, jnp.concatenate([a, b], 0), jnp.concatenate([b, a], 0)
            ),
            one,
            two,
        )

    def embedding_far(keep, send):
        keep, send = quarters_of(keep + swap(send, "mp", mp, 1))
        return keep, swap(half_float(send), "mp", mp, 2)

    def own_embedding(keep, far):
        grad, sums, limit = embedding(keep, float_half(far))
        return half_float(grad, limit[0, 0]), sums, limit

    def all_embedding(sent, far):
        sent = ordered(sent, far, high_bit)
        near = swap(sent, "mp", mp, 1)
        values, scales = jax.tree.map(lambda a, b: jnp.concatenate([a, b], 0), sent, near)
        whole = values.astype(f32).reshape(mp, share, D) * scales[:, :1, None]
        whole = whole.reshape(tokens, D)
        return split(whole, 2)

    def vector_of(sums_zero, limit):
        def spread(part, width, start):
            return lax.dynamic_update_slice_in_dim(jnp.zeros((1, width), f32), part, start, 1)

        bound = share * limit[:, :1] + rank_first * count * top_feature[:, :1]
        return jnp.concatenate(
            [
                sums_zero,
                spread(query_sums, D, model_rank * inner),
                spread(keyval_sums[:, inner:], D, model_rank * inner),
                sums_one[2:3] * rank_first,
                sums_one[0:2] * rank_first,
                spread(upper_sums, FF, model_rank * hidden).reshape(ff_rows, D),
                sums_two[2:3] * rank_first,
                sums_two[0:2] * rank_first,
                jnp.concatenate(
                    [
                        jnp.broadcast_to(loss_part[:, :1] * rank_first, (1, D // 2)),
                        jnp.broadcast_to(bound, (1, D // 2)),
                    ],
                    axis=1,
                ),
            ],
            axis=0,
        )

    place_rows = LEN // mp
    per_owner = place_rows // dp
    place_codes = offset.reshape(1, -1) - model_rank * place_rows
    place_codes = jnp.where(
        (place_codes >= 0) & (place_codes < place_rows),
        place_of(place_codes // per_owner) * per_owner + place_codes % per_owner,
        -1,
    )

    def place_gradient(upper, lower):
        return call(
            place_kernel,
            shape((place_rows, D)),
            [],
            [place_codes, upper, lower],
            "place_gradient",
        )

    def shampoo_products(total):
        scale = power_scale(jnp.max(jnp.abs(total)))
        gradient = total[None] / scale
        return (
            scale,
            jnp.einsum("...ij,...kj->...ik", gradient, gradient, precision=HIGH),
            jnp.einsum("...ji,...jk->...ik", gradient, gradient, precision=HIGH),
            jnp.einsum(
                "...ij,...jk->...ik",
                jnp.einsum("...ij,...jk->...ik", root_left, gradient, precision=HIGH),
                root_right,
                precision=HIGH,
            ),
        )

    def reduce_step(parts, k, moving, kind, beside):
        met = along_x(parts[2 * k + 1].astype(kind))
        if moving is None:
            met, beside = fence(met, beside)
            return parts[2 * k].astype(f32) + met.astype(f32), beside
        came = ring_step(moving.astype(kind))
        met, came, beside = fence(met, came, beside)
        return parts[2 * k].astype(f32) + came.astype(f32) + met.astype(f32), beside

    if fast:
        total, far = reduce_step(layer_grad, 1, None, bf16, embedding_far(keep, send))
        keep, far = far
        sent, sums_zero, limit_here = own_embedding(keep, far)
        far = swap(sent, "mp", mp, 2)
        total, beside = reduce_step(
            layer_grad, 2, total, bf16, (sent, far, sums_zero, limit_here)
        )
        sent, far, sums_zero, limit_here = beside
        upper, lower = all_embedding(sent, far)
        vector_part = vector_of(sums_zero, limit_here)
        vector_part = near_sum(vector_part, dp, mp)
        total, beside = reduce_step(
            layer_grad, 3, total, bf16, (upper, lower, vector_part)
        )
        upper, lower, vector_part = beside
        vector_part = far_sum(vector_part, dp)
        place_grad = place_gradient(upper, lower)
        table_grad = table_gradient(codes[None], upper, lower, grad_logits, picked_low)
        layer_total, beside = reduce_step(
            layer_grad, 0, total, bf16, (vector_part, place_grad, table_grad)
        )
        vector_part, place_grad, table_grad = beside
        scale_all = power_scale(vector_part[-1, D // 2])
        inverse = 1.0 / scale_all

        parts = table_grad.reshape(dp, VOC_PAD, D)[:, :VOC_DEV] * inverse
        place_sent = (place_grad.reshape(dp, per_owner, D) * inverse).astype(f16)
        arrived = [place_sent[0]]
        for r in range(1, dp):
            pairs = [
                (i, 2 * ((i // 2 - r // 2) % RING) + (i % 2 + r % 2) % 2) for i in range(dp)
            ]
            arrived.append(lax.ppermute(place_sent[r], "dp", pairs))
        layer_scale, gram_left, gram_right, shaped = shampoo_products(layer_total)
        total, arrived = reduce_step(parts, 1, None, f16, arrived)
        place_total = sum(one.astype(f32) for one in arrived)
        sent = place_total.astype(f16)
        steps = [sent]
        for shift in range(1, RING):
            pairs = [(i, (i + 2 * shift) % dp) for i in range(dp)]
            steps.append(lax.ppermute(sent, "dp", pairs))
        total, beside = reduce_step(parts, 2, total, f16, (steps, place_total, gram_left))
        steps, place_total, gram_left = beside
        steps = jnp.stack(steps[::-1] * 2)
        steps = lax.dynamic_slice_in_dim(steps, (RING - 1 - z_here) % RING, RING, 0)
        near = along_x(steps)
        total, beside = reduce_step(parts, 3, total, f16, (steps, near, gram_right))
        steps, near, gram_right = beside

        def sided(one, two, bit):
            return jnp.where(bit == 0, jnp.stack([one, two]), jnp.stack([two, one]))

        place_all = sided(steps, near, x_here).transpose(1, 0, 2, 3)
        place_all = place_all.reshape(place_rows, D)
        near = swap(place_all, "mp", mp, 2)
        table_total, beside = reduce_step(
            parts, 0, total, f16, (place_all, near, shaped)
        )
        place_all, near, shaped = beside
        table_total = table_total * scale_all
        place_total = place_total * scale_all
        place_all = sided(place_all, near, high_bit)
        place_all = sided(place_all, swap(place_all, "mp", mp, 1), low_bit)
        place_sum = place_all.transpose(1, 0, 2, 3).reshape(LEN, D).astype(f32) * scale_all
    else:
        layer_total = lax.psum_scatter(
            layer_grad[0].astype(f32), "dp", scatter_dimension=0, tiled=True
        )
        layer_scale, gram_left, gram_right, shaped = shampoo_products(layer_total)
        sent, sums_zero, limit_here = own_embedding(*embedding_far(keep, send))
        upper, lower = all_embedding(sent, swap(sent, "mp", mp, 2))
        vector_part = butterfly(vector_of(sums_zero, limit_here), jnp.add, dp, mp)
        table_grad = table_gradient(codes[None], upper, lower, grad_logits, picked_low)
        table_total = lax.psum_scatter(table_grad, "dp", scatter_dimension=0, tiled=True)[:VOC_DEV]
        place_total = lax.psum_scatter(
            place_gradient(upper, lower), "dp", scatter_dimension=0, tiled=True
        )
        place_sum = lax.all_gather(
            lax.all_gather(place_total, "dp", axis=0, tiled=True), "mp", axis=0, tiled=True
        )
    tail_sum, loss_sum = vector_part[:-1], vector_part[-1, 0]

    squares = (
        jnp.sum(layer_total * layer_total)
        + jnp.sum(table_total * table_total)
        + jnp.sum(place_total * place_total)
    )
    squares = jnp.broadcast_to(squares, (1, 128))
    if fast:
        squares = far_sum(near_sum(squares, dp, mp), dp)[0, 0]
    else:
        squares = butterfly(squares, jnp.add, dp, mp)[0, 0]
    squares = squares + jnp.sum(tail_sum * tail_sum)
    grad_norm = jnp.sqrt(squares)
    count_all = rows * dp * POS
    limit = CLIP_FACTOR * math.sqrt(count_all)
    factor = jnp.minimum(1.0, limit / grad_norm)
    shrink = factor * layer_scale

    left_new = STAT_DECAY * stats_left + (1.0 - STAT_DECAY) * (shrink * shrink) * gram_left
    right_new = STAT_DECAY * stats_right + (1.0 - STAT_DECAY) * (shrink * shrink) * gram_right
    layer_new = layer_master - RATE_SHAMPOO * (shaped * shrink + DECAY_LAYER * layer_master)

    table_new, table_one, table_two = adam_step(
        table_master, table_first, table_second, table_total * factor, DECAY_TABLE
    )
    vector_sum = jnp.concatenate([place_sum, tail_sum], axis=0)
    vector_new, vector_one, vector_two = adam_step(
        vector_master, vector_first, vector_second, vector_sum * factor, 0.0
    )
    loss = loss_sum / f32(count_all)
    return (
        loss,
        grad_norm,
        layer_new,
        left_new,
        right_new,
        table_new,
        table_one,
        table_two,
        vector_new,
        vector_one,
        vector_two,
    )


def solution(mesh):
    blocks = P("mp", "dp", None, None)
    vocab = P(("dp", "mp"), None)
    rows = P("dp", None)
    return jax.shard_map(
        local,
        mesh=mesh,
        in_specs=(rows,) * 4 + (P(),) + (blocks,) * 5 + (vocab,) * 3 + (P(),) * 3,
        out_specs=(P(), P()) + (blocks,) * 3 + (vocab,) * 3 + (P(),) * 3,
        check_vma=False,
    )
```

time: 640 us -> 499 us (0.78)
  Pallas kernels: 17.3 us -> 87.3 us
  matrix products: 89.2 us -> 27.6 us
  other arithmetic: 115 us -> 67.7 us
  local copies, waits for them, and re-layouts: 70.8 us -> 29 us
  blocking collectives: 33.4 us -> 0 us
  waiting for transfers between devices: 207 us -> 193 us
  between operations: 23.3 us -> 11.4 us
    pallas_call x2 -> x14, Pallas kernels: 17.3 us -> 87.3 us  [the longest x12 65.4 us: call(): pl.pallas_call(kernel, out_shape=outs, in_specs=[SMEM] * len(scalars) + [...]
    dot_general x27 -> x4, matrix products: 71.4 us -> 18.4 us  [the longest x1 6.33 us: shampoo_products(): jnp.einsum('...ij,...kj->...ik', gradient, gradient, precision=HIGH)]
    all_gather x1 -> x0, blocking collectives: 33.4 us -> none  [local(): lax.all_gather(place_total, 'dp', axis=0, tiled=True)]
    ppermute x24 -> x12, waiting for transfers between devices: 50.3 us -> 17.5 us  [ring_step(): return lax.ppermute(value, 'dp', pairs)]
    reshape x12 -> x3, local copies, waits for them, and re-layouts: 23.7 us -> 1.42 us  [the longest x1 0.79 us: local(): pick_segment = jnp.sum((seq_ends_of(seq_lengths)[:, None, :] <= loss_posi...]
    unnamed x16 -> x3, other arithmetic: 20.7 us -> 0.03 us
    ppermute x70 -> x58, waiting for transfers between devices: 157 us -> 176 us  [swap(): return jax.tree.map(lambda part: lax.ppermute(part, axis, pairs), value)]
    ppermute x0 -> x10, starting transfers between devices: none -> 15.9 us  [the longest x7 11.3 us: local(): arrived.append(lax.ppermute(place_sent[r], 'dp', pairs))]
  transfers between devices with their start and end apart: 95 -> 80, of which waited for: 61 -> 38; matrix products, arithmetic and copies ran while one was open for 25% -> 20% of each run, Pallas kernels for 3% -> 8%
where the time goes in v2:
time: 499 us; the launch traced here: 490 us
  waiting for transfers between devices  193 us (39%)
  Pallas kernels  87.3 us (17%)
  starting transfers between devices  74.2 us (15%)
  other arithmetic  67.7 us (14%)
  local copies, waits for them, and re-layouts  29 us (6%)
  matrix products  27.6 us (6%)
  between operations  11.4 us (2%)
    ppermute x58, waiting for transfers between devices, swap(): return jax.tree.map(lambda part: lax.ppermute(part, axis, pairs), value)  176 us
    pallas_call x12, Pallas kernels, call(): pl.pallas_call(kernel, out_shape=outs, in_specs=[SMEM] * len(scalars) + [...  65.4 us
    ppermute x58, starting transfers between devices, swap(): return jax.tree.map(lambda part: lax.ppermute(part, axis, pairs), value)  50.9 us
    ppermute x12, waiting for transfers between devices, ring_step(): return lax.ppermute(value, 'dp', pairs)  17.5 us
    pallas_call x1, Pallas kernels, table_gradient(): pl.pallas_call(table_kernel, grid=(vocab // STRIP, D // wide), out_shape=...  12.4 us
    ppermute x7, starting transfers between devices, local(): arrived.append(lax.ppermute(place_sent[r], 'dp', pairs))  11.3 us
    unnamed x144, local copies, waits for them, and re-layouts  10.9 us
  transfers between devices with their start and end apart: 80, of which 38 were waited for; matrix products, arithmetic and copies ran while one was open for 20% of the time, Pallas kernels for 8%

profile of v2, /device:TPU:0, one launch (start us, length us, event | category | flops | bytes accessed | tf_op | source)
XLA Modules:
  0.0 490.4 jit_solution(6996270091448891949)
XLA Ops:
  21.5 7.1 %collective-permute-done.3.refs_3_ = bf16[208,1024]{1,0:T(8,128)(2,1)S(1)} collective-permute-done((bf16[208,1024]{1,0:T(8,128)(2,1)S(1)}, bf16[208,1024]{1,0:T(8,128)(2,1)S(1)}, u32[]{:S(2)}, u32[]{:S(2)}) %collective-permute-start.3) | collective-permute-done | bytes 426016 | tf_op jit(solution)/shard_map/ppermute | solution.py:45
  32.3 8.1 %collective-permute-done.5.refs_5_ = bf16[208,1024]{1,0:T(8,128)(2,1)S(1)} collective-permute-done((bf16[208,1024]{1,0:T(8,128)(2,1)S(1)}, bf16[208,1024]{1,0:T(8,128)(2,1)S(1)}, u32[]{:S(2)}, u32[]{:S(2)}) %collective-permute-start.5) | collective-permute-done | bytes 426016 | tf_op jit(solution)/shard_map/ppermute | solution.py:45
  46.0 22.1 %collective-permute-done.8.refs_7_ = bf16[208,1024]{1,0:T(8,128)(2,1)} collective-permute-done((bf16[208,1024]{1,0:T(8,128)(2,1)S(1)}, bf16[208,1024]{1,0:T(8,128)(2,1)}, u32[]{:S(2)}, u32[]{:S(2)}) %collective-permute-start.8) | collective-permute-done | bytes 426016 | tf_op jit(solution)/shard_map/ppermute | solution.py:45
  68.1 5.1 %embed.3 = bf16[512,1024]{1,0:T(8,128)(2,1)} custom-call(s32[512,1]{1,0:T(8,128)} %copy.83.codes, bf16[208,1024]{1,0:T(8,128)(2,1)} %copy-done.5, bf16[208,1024]{1,0:T(8,128)(2,1)} %copy-done.6, bf16[208,1024]{1,0:T(8,128)(2,1)} %copy-done.7, bf16[208,1024]{1,0:T(8,128)(2,1)} %copy-done.8, bf16[208,1024]{1,0:T(8,128)(2,1)} %copy-done.9, ...), custom_call_target="tpu_custom_call" | custom-call | flops 1 | bytes 1 | tf_op jit(solution)/shard_map/embed/pallas_call | solution.py:220
  75.4 5.1 %embed.2 = bf16[512,1024]{1,0:T(8,128)(2,1)} custom-call(s32[512,1]{1,0:T(8,128)} %copy.82.codes, bf16[208,1024]{1,0:T(8,128)(2,1)} %copy-done.5, bf16[208,1024]{1,0:T(8,128)(2,1)} %copy-done.6, bf16[208,1024]{1,0:T(8,128)(2,1)} %copy-done.7, bf16[208,1024]{1,0:T(8,128)(2,1)} %copy-done.8, bf16[208,1024]{1,0:T(8,128)(2,1)} %copy-done.9, ...), custom_call_target="tpu_custom_call" | custom-call | flops 1 | bytes 1 | tf_op jit(solution)/shard_map/embed/pallas_call | solution.py:220
  82.4 11.0 %collective-permute-done.10.refs_3_ = bf16[24,128,128]{2,1,0:T(8,128)(2,1)S(1)} collective-permute-done((bf16[24,128,128]{2,1,0:T(8,128)(2,1)}, bf16[24,128,128]{2,1,0:T(8,128)(2,1)S(1)}, u32[]{:S(2)}, u32[]{:S(2)}) %collective-permute-start.10) | collective-permute-done | bytes 786464 | tf_op jit(solution)/shard_map/ppermute | solution.py:45
  98.8 17.2 %collective-permute-done.13.refs_5_ = bf16[24,128,128]{2,1,0:T(8,128)(2,1)} collective-permute-done((bf16[24,128,128]{2,1,0:T(8,128)(2,1)}, bf16[24,128,128]{2,1,0:T(8,128)(2,1)}, u32[]{:S(2)}, u32[]{:S(2)}) %collective-permute-start.13) | collective-permute-done | bytes 786464 | tf_op jit(solution)/shard_map/ppermute | solution.py:45
  138.2 8.8 %collective-permute-done.15.refs_7_ = bf16[24,128,128]{2,1,0:T(8,128)(2,1)} collective-permute-done((bf16[24,128,128]{2,1,0:T(8,128)(2,1)}, bf16[24,128,128]{2,1,0:T(8,128)(2,1)}, u32[]{:S(2)}, u32[]{:S(2)}) %collective-permute-start.15) | collective-permute-done | bytes 786464 | tf_op jit(solution)/shard_map/ppermute | solution.py:45
  146.9 9.5 %attend.1 = (bf16[1024,768]{1,0:T(8,128)(2,1)}, bf16[256,1024]{1,0:T(8,128)(2,1)}, bf16[1024,1024]{1,0:T(8,128)(2,1)}, bf16[1024,1024]{1,0:T(8,128)(2,1)}, bf16[...) custom-call(s32[192]{0:T(256)} %get-tuple-element.353.downs, ...), custom_call_target="tpu_custom_call" | custom-call | flops 1 | bytes 1 | tf_op jit(solution)/shard_map/attend/pallas_call | solution.py:442
  160.2 9.0 %collective-permute-done.18 = f32[80,1024]{1,0:T(8,128)S(1)} collective-permute-done((f32[80,1024]{1,0:T(8,128)S(1)}, f32[80,1024]{1,0:T(8,128)S(1)}, u32[]{:S(2)}, u32[]{:S(2)}) %collective-permute-start.18) | collective-permute-done | bytes 327712 | tf_op jit(solution)/shard_map/ppermute | solution.py:45
  181.5 9.2 %collective-permute-done.21 = f32[80,1024]{1,0:T(8,128)S(1)} collective-permute-done((f32[80,1024]{1,0:T(8,128)S(1)}, f32[80,1024]{1,0:T(8,128)S(1)}, u32[]{:S(2)}, u32[]{:S(2)}) %collective-permute-start.21) | collective-permute-done | bytes 327712 | tf_op jit(solution)/shard_map/ppermute | solution.py:45
  193.2 5.6 %logits.1 = (f32[160,1024]{1,0:T(8,128)}, f32[160,1]{1,0:T(8,128)}, bf16[160,1024]{1,0:T(8,128)(2,1)}, f32[1,128]{1,0:T(1,128)}, f32[1664,160]{1,0:T(8,128)}, /*index=5*/f32[8,160]{1,0:T(8,128)}) custom-call(f32[80,1024]{1,0:T(8,128)} %copy-done.29, f32[80,1024]{1,0:T(8,128)} %copy-done.43, f32[160,1024]{1,0:T(8,128)} %get-tuple-element.194.first, ...), custom_call_target="tpu_custom_call" | custom-call | flops 1 | bytes 1 | tf_op jit(solution)/shard_map/logits/pallas_call | solution.py:220
  212.6 8.5 %collective-permute-done.27 = f32[80,1024]{1,0:T(8,128)S(1)} collective-permute-done((f32[80,1024]{1,0:T(8,128)S(1)}, f32[80,1024]{1,0:T(8,128)S(1)}, u32[]{:S(2)}, u32[]{:S(2)}) %collective-permute-start.27) | collective-permute-done | bytes 327712 | tf_op jit(solution)/shard_map/ppermute | solution.py:45
  223.5 5.6 %backward.1 = (f32[160,1024]{1,0:T(8,128)}, bf16[160,1024]{1,0:T(8,128)(2,1)}, bf16[160,1024]{1,0:T(8,128)(2,1)}, f32[3,1024]{1,0:T(4,128)}, f32[1,1024]{1,0:T(1...) custom-call(f32[80,1024]{1,0:T(8,128)} %copy-done.30, f32[80,1024]{1,0:T(8,128)} %copy-done.44, ...), custom_call_target="tpu_custom_call" | custom-call | flops 1 | bytes 1 | tf_op jit(solution)/shard_map/backward/pallas_call | solution.py:220
  233.3 8.5 %collective-permute-done.30 = f32[80,1024]{1,0:T(8,128)S(1)} collective-permute-done((f32[80,1024]{1,0:T(8,128)S(1)}, f32[80,1024]{1,0:T(8,128)S(1)}, u32[]{:S(2)}, u32[]{:S(2)}) %collective-permute-start.30) | collective-permute-done | bytes 327712 | tf_op jit(solution)/shard_map/ppermute | solution.py:45
  244.2 11.0 %back_attention.1 = (f32[512,1024]{1,0:T(8,128)}, f32[512,1024]{1,0:T(8,128)}, f32[3,1024]{1,0:T(4,128)}, f32[1,256]{1,0:T(1,128)}, f32[1,512]{1,0:T(1,128)}, /*...) custom-call(s32[160]{0:T(256)} %reshape.1241.positions, f32[1]{0:T(128)} %bitcast.10.rank_first, ...), custom_call_target="tpu_custom_call" | custom-call | flops 1 | bytes 1 | tf_op jit(solution)/shard_map/back_attention/pallas_call | solution.py:220
  258.9 8.1 %back_weights.1 = (bf16[24,128,128]{2,1,0:T(8,128)(2,1)}, bf16[24,128,128]{2,1,0:T(8,128)(2,1)}, bf16[24,128,128]{2,1,0:T(8,128)(2,1)}, bf16[24,128,128]{2,1,0:T...) custom-call(s32[192]{0:T(256)} %get-tuple-element.353.downs, ...), custom_call_target="tpu_custom_call" | custom-call | flops 1 | bytes 1 | tf_op jit(solution)/shard_map/back_weights/pallas_call | solution.py:220
  281.8 5.9 %collective-permute-done.35 = bf16[24,128,128]{2,1,0:T(8,128)(2,1)} collective-permute-done((bf16[24,128,128]{2,1,0:T(8,128)(2,1)}, bf16[24,128,128]{2,1,0:T(8,128)(2,1)}, u32[]{:S(2)}, u32[]{:S(2)}) %collective-permute-start.35) | collective-permute-done | bytes 786464 | tf_op jit(solution)/shard_map/ppermute | solution.py:45
  302.9 17.9 %collective-permute-done.34 = bf16[24,128,128]{2,1,0:T(8,128)(2,1)} collective-permute-done((bf16[24,128,128]{2,1,0:T(8,128)(2,1)}, bf16[24,128,128]{2,1,0:T(8,128)(2,1)}, u32[]{:S(2)}, u32[]{:S(2)}) %collective-permute-start.34) | collective-permute-done | bytes 786464 | tf_op jit(solution)/shard_map/ppermute | solution.py:45
  332.1 18.6 %collective-permute-done.48 = f32[15,1024]{1,0:T(8,128)S(1)} collective-permute-done((f32[15,1024]{1,0:T(8,128)S(1)}, f32[15,1024]{1,0:T(8,128)S(1)}, u32[]{:S(2)}, u32[]{:S(2)}) %collective-permute-start.48) | collective-permute-done | bytes 61472 | tf_op jit(solution)/shard_map/ppermute | solution.py:45
  364.0 12.4 %table_gradient.1 = f32[1664,1024]{1,0:T(8,128)} custom-call(s32[1,1024]{1,0:T(1,128)} %get-tuple-element.354.codes, bf16[1024,1024]{1,0:T(8,128)(2,1)} %get-tuple-element.254.upper, bf16[1024,1024]{1,0:T(8,128)(2,1)} %get-tuple-element.255.lower, bf16[1664,160]{1,0:T(8,128)(2,1)} %get-tuple-element.256.grad_logits, ...), custom_call_target="tpu_custom_call" | custom-call | flops 1 | bytes 1 | tf_op jit(solution)/shard_map/table_gradient/pallas_call | solution.py:758
  387.3 7.3 %fusion.86 = (f16[8,197,1024]{2,1,0:T(8,128)(2,1)S(1)}, f32[8,197,1024]{2,1,0:T(8,128)}) fusion(f32[]{:T(128)S(6)} %div.273, f32[8,208,1024]{2,1,0:T(8,128)} %bitcast.141), kind=kLoop, calls=%fused_computation.306 | loop fusion | flops 3227648 | bytes 16138244 | tf_op jit(solution)/shard_map/convert.3
  417.1 6.3 %convolution_bitcast_fusion.1 = f32[1,24,128,128]{3,2,1,0:T(8,128)} fusion(f32[]{:T(128)S(6)} %exp2.31, bf16[24,128,128]{2,1,0:T(8,128)(2,1)S(1)} %collective-permute-done.32, bf16[24,128,128]{2,1,0:T(8,128)(2,1)} %collective-permute-done.49, bf16[24,128,128]{2,1,0:T(8,128)(2,1)S(1)} %copy-done.34), kind=kOutput, calls=%fused_computation.36 | convolution fusion | flops 606339072 | bytes 3932164 | tf_op jit(solution)/shard_map/...ij,...kj->...ik/dot_general | solution.py:1154
  428.8 5.7 %convolution_bitcast_fusion = f32[1,24,128,128]{3,2,1,0:T(8,128)} fusion(f32[]{:T(128)S(6)} %exp2.31, bf16[24,128,128]{2,1,0:T(8,128)(2,1)S(1)} %collective-permute-done.32, bf16[24,128,128]{2,1,0:T(8,128)(2,1)} %collective-permute-done.49, bf16[24,128,128]{2,1,0:T(8,128)(2,1)S(1)} %copy-done.34), kind=kOutput, calls=%fused_computation.35 | convolution fusion | flops 606339072 | bytes 3932164 | tf_op jit(solution)/shard_map/...ji,...jk->...ik/dot_general | solution.py:1155
  (426 shorter events, 245.6 us)
Async XLA Ops:
  42.9 25.2 %collective-permute-start.7 = (bf16[24,128,128]{2,1,0:T(8,128)(2,1)}, bf16[24,128,128]{2,1,0:T(8,128)(2,1)}, u32[]{:S(2)}, u32[]{:S(2)}) collective-permute-start(bf16[24,128,128]{2,1,0:T(8,128)(2,1)} %convert_bitcast_fusion.refs_0_), channel_id=1, source_target_pairs={{0,4},{4,0},{8,12},{12,8},{16,20},{20,16},{24,28},{28,24},{1,5},{5... | collective-permute-start | bytes 2359304 | tf_op jit(solution)/shard_map/ppermute | solution.py:45
  43.9 24.2 %collective-permute-start.6 = (bf16[24,128,128]{2,1,0:T(8,128)(2,1)}, bf16[24,128,128]{2,1,0:T(8,128)(2,1)}, u32[]{:S(2)}, u32[]{:S(2)}) collective-permute-start(bf16[24,128,128]{2,1,0:T(8,128)(2,1)} %convert_bitcast_fusion.refs_0_), channel_id=1, source_target_pairs={{0,8},{4,12},{8,16},{12,20},{16,24},{20,28},{24,0},{28,4},{1,9},{5... | collective-permute-start | bytes 2359304 | tf_op jit(solution)/shard_map/ppermute | solution.py:50
  44.0 24.1 %collective-permute-start.8 = (bf16[208,1024]{1,0:T(8,128)(2,1)S(1)}, bf16[208,1024]{1,0:T(8,128)(2,1)}, u32[]{:S(2)}, u32[]{:S(2)}) collective-permute-start(bf16[208,1024]{1,0:T(8,128)(2,1)S(1)} %collective-permute-done.4.refs_6_), channel_id=1, source_target_pairs={{0,4},{4,0},{8,12},{12,8},{16,20},{20,16},{24,28},{28,24},{1,5},{5... | collective-permute-start | bytes 1277960 | tf_op jit(solution)/shard_map/ppermute | solution.py:45
  73.2 20.2 %collective-permute-start.10 = (bf16[24,128,128]{2,1,0:T(8,128)(2,1)}, bf16[24,128,128]{2,1,0:T(8,128)(2,1)S(1)}, u32[]{:S(2)}, u32[]{:S(2)}) collective-permute-start(bf16[24,128,128]{2,1,0:T(8,128)(2,1)} %collective-permute-done.6.refs_2_), channel_id=1, source_target_pairs={{0,4},{4,0},{8,12},{12,8},{16,20},{20,16},{24,28},{28,24},{1,5},{5... | collective-permute-start | bytes 2359304 | tf_op jit(solution)/shard_map/ppermute | solution.py:45
  74.5 21.8 %collective-permute-start.9 = (bf16[24,128,128]{2,1,0:T(8,128)(2,1)}, bf16[24,128,128]{2,1,0:T(8,128)(2,1)}, u32[]{:S(2)}, u32[]{:S(2)}) collective-permute-start(bf16[24,128,128]{2,1,0:T(8,128)(2,1)} %collective-permute-done.6.refs_2_), channel_id=1, source_target_pairs={{0,8},{4,12},{8,16},{12,20},{16,24},{20,28},{24,0},{28,4},{1,9},{5... | collective-permute-start | bytes 2359304 | tf_op jit(solution)/shard_map/ppermute | solution.py:50
  96.3 24.6 %collective-permute-start.14 = (bf16[512,1024]{1,0:T(8,128)(2,1)S(1)}, bf16[512,1024]{1,0:T(8,128)(2,1)}, u32[]{:S(2)}, u32[]{:S(2)}) collective-permute-start(bf16[512,1024]{1,0:T(8,128)(2,1)S(1)} %add.760), channel_id=1, source_target_pairs={{0,2},{1,3},{2,0},{3,1},{4,6},{5,7},{6,4},{7,5},{8,10},{9,11},{10,... | collective-permute-start | bytes 3145736 | tf_op jit(solution)/shard_map/ppermute | solution.py:45
  98.6 20.6 %collective-permute-start.12 = (bf16[24,128,128]{2,1,0:T(8,128)(2,1)}, bf16[24,128,128]{2,1,0:T(8,128)(2,1)}, u32[]{:S(2)}, u32[]{:S(2)}) collective-permute-start(bf16[24,128,128]{2,1,0:T(8,128)(2,1)} %collective-permute-done.9.refs_4_), channel_id=1, source_target_pairs={{0,8},{4,12},{8,16},{12,20},{16,24},{20,28},{24,0},{28,4},{1,9},{5... | collective-permute-start | bytes 2359304 | tf_op jit(solution)/shard_map/ppermute | solution.py:50
  126.7 20.2 %collective-permute-start.15 = (bf16[24,128,128]{2,1,0:T(8,128)(2,1)}, bf16[24,128,128]{2,1,0:T(8,128)(2,1)}, u32[]{:S(2)}, u32[]{:S(2)}) collective-permute-start(bf16[24,128,128]{2,1,0:T(8,128)(2,1)} %collective-permute-done.12.refs_6_), channel_id=1, source_target_pairs={{0,4},{4,0},{8,12},{12,8},{16,20},{20,16},{24,28},{28,24},{1,5},{5... | collective-permute-start | bytes 2359304 | tf_op jit(solution)/shard_map/ppermute | solution.py:45
  267.0 20.7 %collective-permute-start.35 = (bf16[24,128,128]{2,1,0:T(8,128)(2,1)}, bf16[24,128,128]{2,1,0:T(8,128)(2,1)}, u32[]{:S(2)}, u32[]{:S(2)}) collective-permute-start(bf16[24,128,128]{2,1,0:T(8,128)(2,1)} %get-tuple-element.226), channel_id=1, source_target_pairs={{0,4},{4,0},{8,12},{12,8},{16,20},{20,16},{24,28},{28,24},{1,5},{5... | collective-permute-start | bytes 2359304 | tf_op jit(solution)/shard_map/ppermute | solution.py:45
  279.7 100.2 %collective-permute-start.32 = (bf16[24,128,128]{2,1,0:T(8,128)(2,1)}, bf16[24,128,128]{2,1,0:T(8,128)(2,1)S(1)}, u32[]{:S(2)}, u32[]{:S(2)}) collective-permute-start(bf16[24,128,128]{2,1,0:T(8,128)(2,1)} %get-tuple-element.220), channel_id=1, source_target_pairs={{0,4},{4,0},{8,12},{12,8},{16,20},{20,16},{24,28},{28,24},{1,5},{5... | collective-permute-start | bytes 2359304 | tf_op jit(solution)/shard_map/ppermute | solution.py:45
  280.3 40.4 %collective-permute-start.34 = (bf16[24,128,128]{2,1,0:T(8,128)(2,1)}, bf16[24,128,128]{2,1,0:T(8,128)(2,1)}, u32[]{:S(2)}, u32[]{:S(2)}) collective-permute-start(bf16[24,128,128]{2,1,0:T(8,128)(2,1)} %get-tuple-element.224), channel_id=1, source_target_pairs={{0,4},{4,0},{8,12},{12,8},{16,20},{20,16},{24,28},{28,24},{1,5},{5... | collective-permute-start | bytes 2359304 | tf_op jit(solution)/shard_map/ppermute | solution.py:45
  292.8 28.8 %collective-permute-start.39 = (bf16[24,128,128]{2,1,0:T(8,128)(2,1)}, bf16[24,128,128]{2,1,0:T(8,128)(2,1)}, u32[]{:S(2)}, u32[]{:S(2)}) collective-permute-start(bf16[24,128,128]{2,1,0:T(8,128)(2,1)} %add_convert_fusion.2), channel_id=1, source_target_pairs={{0,8},{4,12},{8,16},{12,20},{16,24},{20,28},{24,0},{28,4},{1,9},{5... | collective-permute-start | bytes 2359304 | tf_op jit(solution)/shard_map/ppermute | solution.py:50
  300.7 20.1 %collective-permute-start.40 = (f16[256,1024]{1,0:T(8,128)(2,1)S(1)}, f16[256,1024]{1,0:T(8,128)(2,1)S(1)}, u32[]{:S(2)}, u32[]{:S(2)}) collective-permute-start(f16[256,1024]{1,0:T(8,128)(2,1)S(1)} %divide_convert_fusion), channel_id=1, source_target_pairs={{0,2},{1,3},{2,0},{3,1},{4,6},{5,7},{6,4},{7,5},{8,10},{9,11},{10,... | collective-permute-start | bytes 1572872 | tf_op jit(solution)/shard_map/ppermute | solution.py:45
  301.3 19.5 %collective-permute-start.41 = (f32[1,128]{1,0:T(1,128)S(1)}, f32[1,128]{1,0:T(1,128)S(1)}, u32[]{:S(2)}, u32[]{:S(2)}) collective-permute-start(f32[1,128]{1,0:T(1,128)S(1)} %broadcast_in_dim.95), channel_id=1, source_target_pairs={{0,2},{1,3},{2,0},{3,1},{4,6},{5,7},{6,4},{7,5},{8,10},{9,11},{10,... | collective-permute-start | bytes 1544 | tf_op jit(solution)/shard_map/ppermute | solution.py:45
  326.3 24.5 %collective-permute-start.43 = (f16[512,1024]{1,0:T(8,128)(2,1)S(1)}, f16[512,1024]{1,0:T(8,128)(2,1)S(1)}, u32[]{:S(2)}, u32[]{:S(2)}) collective-permute-start(f16[512,1024]{1,0:T(8,128)(2,1)S(1)} %maximum_select_fusion), channel_id=1, source_target_pairs={{0,1},{1,0},{2,3},{3,2},{4,5},{5,4},{6,7},{7,6},{8,9},{9,8},{10,11... | collective-permute-start | bytes 3145736 | tf_op jit(solution)/shard_map/ppermute | solution.py:45
  329.7 24.0 %collective-permute-start.33 = (bf16[24,128,128]{2,1,0:T(8,128)(2,1)S(1)}, bf16[24,128,128]{2,1,0:T(8,128)(2,1)S(1)}, u32[]{:S(2)}, u32[]{:S(2)}) collective-permute-start(bf16[24,128,128]{2,1,0:T(8,128)(2,1)S(1)} %copy-done.60), channel_id=1, source_target_pairs={{0,4},{4,0},{8,12},{12,8},{16,20},{20,16},{24,28},{28,24},{1,5},{5... | collective-permute-start | bytes 2359304 | tf_op jit(solution)/shard_map/ppermute | solution.py:45
  331.2 22.4 %collective-permute-start.42 = (bf16[24,128,128]{2,1,0:T(8,128)(2,1)S(1)}, bf16[24,128,128]{2,1,0:T(8,128)(2,1)S(1)}, u32[]{:S(2)}, u32[]{:S(2)}) collective-permute-start(bf16[24,128,128]{2,1,0:T(8,128)(2,1)S(1)} %add_convert_fusion.1), channel_id=1, source_target_pairs={{0,8},{4,12},{8,16},{12,20},{16,24},{20,28},{24,0},{28,4},{1,9},{5... | collective-permute-start | bytes 2359304 | tf_op jit(solution)/shard_map/ppermute | solution.py:50
  331.4 19.3 %collective-permute-start.48 = (f32[15,1024]{1,0:T(8,128)S(1)}, f32[15,1024]{1,0:T(8,128)S(1)}, u32[]{:S(2)}, u32[]{:S(2)}) collective-permute-start(f32[15,1024]{1,0:T(8,128)S(1)} %add_add_fusion.3), channel_id=1, source_target_pairs={{0,4},{4,0},{8,12},{12,8},{16,20},{20,16},{24,28},{28,24},{1,5},{5... | collective-permute-start | bytes 184328 | tf_op jit(solution)/shard_map/ppermute | solution.py:45
  354.9 25.1 %collective-permute-start.49 = (bf16[24,128,128]{2,1,0:T(8,128)(2,1)}, bf16[24,128,128]{2,1,0:T(8,128)(2,1)}, u32[]{:S(2)}, u32[]{:S(2)}) collective-permute-start(bf16[24,128,128]{2,1,0:T(8,128)(2,1)} %add_convert_fusion), channel_id=1, source_target_pairs={{0,8},{4,12},{8,16},{12,20},{16,24},{20,28},{24,0},{28,4},{1,9},{5... | collective-permute-start | bytes 2359304 | tf_op jit(solution)/shard_map/ppermute | solution.py:50
  355.0 23.6 %collective-permute-start.52 = (f32[15,1024]{1,0:T(8,128)S(1)}, f32[15,1024]{1,0:T(8,128)S(1)}, u32[]{:S(2)}, u32[]{:S(2)}) collective-permute-start(f32[15,1024]{1,0:T(8,128)S(1)} %add.791), channel_id=1, source_target_pairs={{0,24},{4,28},{8,16},{12,20},{16,8},{20,12},{24,0},{28,4},{1,25},{... | collective-permute-start | bytes 184328 | tf_op jit(solution)/shard_map/ppermute | solution.py:45
  358.8 21.1 %collective-permute-start.51 = (f32[15,1024]{1,0:T(8,128)S(1)}, f32[15,1024]{1,0:T(8,128)S(1)}, u32[]{:S(2)}, u32[]{:S(2)}) collective-permute-start(f32[15,1024]{1,0:T(8,128)S(1)} %add.791), channel_id=1, source_target_pairs={{0,16},{4,20},{8,24},{12,28},{16,0},{20,4},{24,8},{28,12},{1,17},{... | collective-permute-start | bytes 184328 | tf_op jit(solution)/shard_map/ppermute | solution.py:45
  358.8 21.1 %collective-permute-start.50 = (f32[15,1024]{1,0:T(8,128)S(1)}, f32[15,1024]{1,0:T(8,128)S(1)}, u32[]{:S(2)}, u32[]{:S(2)}) collective-permute-start(f32[15,1024]{1,0:T(8,128)S(1)} %add.791), channel_id=1, source_target_pairs={{0,8},{4,12},{8,0},{12,4},{16,24},{20,28},{24,16},{28,20},{1,9},{5... | collective-permute-start | bytes 184328 | tf_op jit(solution)/shard_map/ppermute | solution.py:45
  382.9 20.0 %collective-permute-start.62 = (f16[16,1024]{1,0:T(8,128)(2,1)}, f16[16,1024]{1,0:T(8,128)(2,1)}, u32[]{:S(2)}, u32[]{:S(2)}) collective-permute-start(f16[16,1024]{1,0:T(8,128)(2,1)} %get-tuple-element.329), channel_id=1, source_target_pairs={{0,8},{4,12},{8,16},{12,20},{16,24},{20,28},{24,0},{28,4},{1,9},{5... | collective-permute-start | bytes 98312 | tf_op jit(solution)/shard_map/ppermute | solution.py:1206
  384.1 20.7 %collective-permute-start.61 = (f16[16,1024]{1,0:T(8,128)(2,1)}, f16[16,1024]{1,0:T(8,128)(2,1)}, u32[]{:S(2)}, u32[]{:S(2)}) collective-permute-start(f16[16,1024]{1,0:T(8,128)(2,1)} %get-tuple-element.330), channel_id=1, source_target_pairs={{0,20},{4,16},{8,28},{12,24},{16,4},{20,0},{24,12},{28,8},{1,21},{... | collective-permute-start | bytes 98312 | tf_op jit(solution)/shard_map/ppermute | solution.py:1206
  (119 other events, 1411.0 us)
